TPU v7x, 128 devices: a whole 4x4x4 slice. The times are simulated.
128 devices in a mesh: node: 16 (over z, x), local: 8 (over y, core).
Axes of the slice: x: 4, y: 4, z: 4, core: 2. Of those that a mesh axis runs over, the one named last changes fastest.
Arguments:
- tokens: bfloat16 [16384, 3584], P(('node', 'local')), may hold values from -6 to 6
- grad_out: bfloat16 [16384, 3584], P(('node', 'local')), may hold values from -6 to 6
- expert_ids: int32 [16384, 1], P(('node', 'local')), may hold values from 0 to 31; in each aligned block of 128 rows (0 to 127, 128 to 255, ...) at most 5 rows name the same one
- route_gate: bfloat16 [16384, 1], P(('node', 'local')), may hold values from 0.25 to 2.5
- expert_gate: bfloat16 [128, 3584, 256], P(('node', 'local')), may hold values from -0.09375 to 0.09375
- expert_up: bfloat16 [128, 3584, 256], P(('node', 'local')), may hold values from -0.09375 to 0.09375
- expert_down: bfloat16 [128, 256, 3584], P(('node', 'local')), may hold values from -0.1875 to 0.1875
- shared_gate: bfloat16 [3584, 1024], P(None, 'local'), may hold values from -0.09375 to 0.09375
- shared_up: bfloat16 [3584, 1024], P(None, 'local'), may hold values from -0.09375 to 0.09375
- shared_down: bfloat16 [1024, 3584], P('local'), may hold values from -0.1875 to 0.1875
Outputs:
- grad_tokens: bfloat16 [16384, 3584], P(('node', 'local'))
- d_expert_gate: bfloat16 [128, 3584, 256], P(('node', 'local'))
- d_expert_up: bfloat16 [128, 3584, 256], P(('node', 'local'))
- d_expert_down: bfloat16 [128, 256, 3584], P(('node', 'local'))
- d_shared_gate: bfloat16 [3584, 1024], P(None, 'local')
- d_shared_up: bfloat16 [3584, 1024], P(None, 'local')
- d_shared_down: bfloat16 [1024, 3584], P('local')
Inputs may be any that keep to these rules, and one draw needn't show every extreme that they name: `expert_ids`: the 128 tokens of one device choose any one expert at most 5 times, and on some devices some expert exactly 5 times.
All inputs are finite; a program needn't handle non-finite values.
Results may differ from a plain program's by a relative error of at most 0.019.
Values may be sent and summed in bfloat16 or wider, within the bound.
No kernel may reach another device: no remote copies, remote signals or barrier semaphores. Data moves between devices by JAX's collectives and lax.ppermute only.
A program may use at most 192 MiB of HBM per device.

v0:
```python
import functools

import jax
import jax.numpy as jnp
from jax import lax
from jax.experimental import pallas as pl
from jax.experimental.pallas import tpu as pltpu
from jax.sharding import Mesh, PartitionSpec as P

CAP = 5
RET = 8
TILE = 512
WEIGHT = {'pack': 8, 'shared_weights': 8, 'routed_rows0': 4, 'routed_rows1': 20, 'routed_weights': 2, 'shared_rows': 20}
F32 = jnp.float32
BF16 = jnp.bfloat16
I32 = jnp.int32
ANY = pl.BlockSpec(memory_space=pl.ANY)
VMEM = pl.BlockSpec(memory_space=pltpu.VMEM)
SMEM = pl.BlockSpec(memory_space=pltpu.SMEM)


def dot(a, b, ca=1, cb=0):
    return lax.dot_general(a, b, (((ca,), (cb,)), ((), ())), preferred_element_type=F32)


def iota(shape, dim):
    return lax.broadcasted_iota(I32, shape, dim)


def hot(cond):
    return jnp.where(cond, 1.0, 0.0).astype(BF16)


def from_y(v, k):
    n = lax.axis_size("y")
    return lax.ppermute(v, "y", [(i, (i - k) % n) for i in range(n)])


def to_y(v, k):
    n = lax.axis_size("y")
    return lax.ppermute(v, "y", [(i, (i + k) % n) for i in range(n)])


def swap_core(v):
    return lax.ppermute(v, "c", [(0, 1), (1, 0)])


def after(v, *earlier):
    return lax.optimization_barrier((v, *earlier))[0]


def call(name, body, outs, operands, specs, scratch, flops, out_specs=None):
    out_shape = [jax.ShapeDtypeStruct(s, d) for s, d in outs]
    size = sum(o.size * o.dtype.itemsize for o in operands)
    size += sum(o.size * o.dtype.itemsize for o in out_shape)
    return pl.pallas_call(
        body,
        out_shape=out_shape,
        in_specs=specs,
        out_specs=out_specs or [VMEM] * len(outs),
        scratch_shapes=scratch,
        compiler_params=pltpu.CompilerParams(vmem_limit_bytes=60 * 2**20),
        name=name,
        cost_estimate=pl.CostEstimate(
            flops=int(flops * WEIGHT.get(name, 1)),
            bytes_accessed=int(size * WEIGHT.get(name, 1)),
            transcendentals=0,
        ),
    )(*operands)


def tile(i):
    return pl.ds(pl.multiple_of(i * TILE, TILE), TILE)


def copies(pairs, sems):
    return [pltpu.make_async_copy(a, b, sems.at[i]) for i, (a, b) in enumerate(pairs)]


def begin(pairs, sems):
    for c in copies(pairs, sems):
        c.start()


def finish(pairs, sems):
    for c in copies(pairs, sems):
        c.wait()


def begin_tiles(pairs_of, count, sems):
    @pl.loop(0, count)
    def _(i):
        begin(pairs_of(i), sems.at[i])


def finish_tiles(pairs_of, count, sems):
    @pl.loop(0, count)
    def _(i):
        finish(pairs_of(i), sems.at[i])


def row_pairs(chunks, held, cols):
    pairs, at = [], 0
    for c in chunks:
        n = c.shape[0]
        pairs.append((c.at[:, cols], held.at[pl.ds(at, n), cols]))
        at += n
    return pairs


def ranks(row):
    n = row.shape[1]
    sub, lane = iota((n, n), 0), iota((n, n), 1)
    col = jnp.sum(jnp.where(sub == lane, row, 0.0), axis=1, keepdims=True)
    same = jnp.where((col == row) & (sub < lane), 1.0, 0.0)
    return jnp.sum(same, axis=0, keepdims=True).astype(I32)


HEAD = 16
BOTH = 2 * CAP


def pack_kernel(where, meta, x, g, out, xv, gv, sems):
    width = xv.shape[1]
    part = width // 4
    tiles = width // TILE
    total, rows = out.shape[0], xv.shape[0]

    def loads(i):
        return [(x.at[:, tile(i)], xv.at[:, tile(i)]), (g.at[:, tile(i)], gv.at[:, tile(i)])]

    begin_tiles(loads, tiles, sems)
    row = meta[0:1, :]
    gate = meta[1:2, :]
    ids = row.astype(I32)
    j = ranks(row) + jnp.where((ids & 1) == where[0] // 2, 0, CAP)
    base = (ids >> 1) * HEAD
    q = iota((total, rows), 0)
    put_x = hot(q == base + j)
    at = jnp.where(j < HEAD - BOTH, base + BOTH + j, -1)
    put_g = jnp.where(q == at, gate, 0.0).astype(BF16)

    @pl.loop(0, tiles)
    def _(i):
        finish(loads(i), sems.at[i])
        cols = tile(i)
        out[:, cols] = (dot(put_x, xv[:, cols]) + dot(put_g, gv[:, cols])).astype(BF16)

    last = None
    for kp in range(4):
        at = jnp.where(j < HEAD - BOTH, -1, base + (j - HEAD + BOTH) * 4 + kp)
        put_t = jnp.where(q == at, gate, 0.0).astype(BF16)
        term = dot(put_t, gv[:, kp * part : (kp + 1) * part])
        last = term if last is None else last + term
    out[:, width:] = last.astype(BF16)


def pack(where, meta, x, g, nodes):
    rows, width = x.shape
    total = nodes * HEAD
    return call(
        "pack",
        pack_kernel,
        [((total, width + width // 4), BF16)],
        [where, meta, x, g],
        [SMEM, VMEM, ANY, ANY],
        [
            pltpu.VMEM((rows, width), BF16),
            pltpu.VMEM((rows, width), BF16),
            pltpu.SemaphoreType.DMA((width // TILE, 2)),
        ],
        2 * total * 3 * rows * width,
    )[0]


def regroup_kernel(msg, near, far):
    total = msg.shape[0]
    width = near.shape[1] // 2
    part = width // 4
    rows = near.shape[0]
    d, q = iota((rows, total), 0), iota((rows, total), 1)
    n = (d * 205) >> 10
    for r, out in enumerate((near, far)):
        j = d - n * CAP + r * CAP
        base = n * HEAD
        get_x = hot(q == base + j)
        get_g = hot((j < HEAD - BOTH) & (q == base + BOTH + j))
        for kp in range(4):
            cols = slice(kp * part, (kp + 1) * part)
            gcols = slice(width + kp * part, width + (kp + 1) * part)
            block = msg[:, cols]
            out[:, cols] = dot(get_x, block).astype(BF16)
            total_g = dot(get_g, block)
            if r == 1:
                get_t = hot((j >= HEAD - BOTH) & (q == base + (j - HEAD + BOTH) * 4 + kp))
                total_g = total_g + dot(get_t, msg[:, width:])
            out[:, gcols] = total_g.astype(BF16)


def regroup(msg, nodes, width):
    return call(
        "regroup",
        regroup_kernel,
        [((nodes * CAP, 2 * width), BF16)] * 2,
        [msg],
        [VMEM],
        [],
        2 * 5 * nodes * CAP * msg.shape[0] * width,
    )


def activations(pre_gate, pre_up, dhidden):
    sig = jax.nn.sigmoid(pre_gate)
    active = pre_gate * sig
    hidden = (active * pre_up).astype(BF16)
    up_in = (dhidden * active).astype(BF16)
    gate_in = (dhidden * pre_up * sig * (1.0 + pre_gate * (1.0 - sig))).astype(BF16)
    return hidden, up_in, gate_in


def weight_pairs(refs, wg, wu, wd, cols):
    go, gs, uo, us, do, ds = refs
    h = do.shape[0]
    own, other = pl.ds(0, h), pl.ds(h, h)
    return [
        (go.at[cols, :], wg.at[cols, own]),
        (gs.at[cols, :], wg.at[cols, other]),
        (uo.at[cols, :], wu.at[cols, own]),
        (us.at[cols, :], wu.at[cols, other]),
        (do.at[:, cols], wd.at[own, cols]),
        (ds.at[:, cols], wd.at[other, cols]),
    ]


def stacked_pairs(refs, wg, wu, wd, cols, i):
    g, u, d, came = refs
    h = d.shape[0]
    own, other = pl.ds(0, h), pl.ds(h, h)
    pairs = [
        (g.at[cols, :], wg.at[cols, own]),
        (came.at[cols, pl.ds(0, h)], wg.at[cols, other]),
        (u.at[cols, :], wu.at[cols, own]),
        (came.at[cols, pl.ds(h, h)], wu.at[cols, other]),
        (d.at[:, cols], wd.at[own, cols]),
    ]
    for c in range(TILE // h):
        at = pl.ds(pl.multiple_of(i * TILE + c * h, h), h)
        pairs.append((came.at[at, pl.ds(2 * h, h)], wd.at[other, at]))
    return pairs


def stack_kernel(g, u, d, out):
    h = g.shape[1]
    out[:, 0:h] = g[...]
    out[:, h : 2 * h] = u[...]
    for c in range(d.shape[1] // h):
        out[c * h : (c + 1) * h, 2 * h :] = d[:, c * h : (c + 1) * h]


def stack(g, u, d):
    width, h = g.shape
    return call("stack", stack_kernel, [((width, 3 * h), BF16)], [g, u, d], [VMEM] * 3, [], 0)[0]


def forward(xv, gv, wg, wu, wd, pg, pu, dh, arrive):
    pg[...] = jnp.zeros_like(pg)
    pu[...] = jnp.zeros_like(pu)
    dh[...] = jnp.zeros_like(dh)

    @pl.loop(0, xv.shape[1] // TILE)
    def _(i):
        arrive(i)
        cols = tile(i)
        x = xv[:, cols]
        pg[...] += dot(x, wg[cols, :])
        pu[...] += dot(x, wu[cols, :])
        dh[...] += dot(gv[:, cols], wd[:, cols], 1, 1)

    return activations(pg[...], pu[...], dh[...])


def shared_rows_kernel(go, uo, came, up_in, gate_in, *refs):
    outs, (wg, wu, held, sems, out_sems) = refs[:4], refs[4:]
    h = go.shape[1]
    own, other = pl.ds(0, h), pl.ds(h, h)

    def loads(i):
        cols = tile(i)
        return [
            (go.at[cols, :], wg.at[cols, own]),
            (came.at[cols, own], wg.at[cols, other]),
            (uo.at[cols, :], wu.at[cols, own]),
            (came.at[cols, other], wu.at[cols, other]),
        ]

    begin_tiles(loads, go.shape[0] // TILE, sems)
    rows_back(gate_in, up_in, wg, wu, outs, held, out_sems, lambda i: finish(loads(i), sems.at[i]))


def rows_back(gate_in, up_in, wg, wu, outs, held, sems, arrive=None):
    rows = outs[0].shape[0]
    tiles = wg.shape[0] // TILE

    def stores(i):
        cols = tile(i)
        return [(held.at[pl.ds(k * rows, rows), cols], o.at[:, cols]) for k, o in enumerate(outs)]

    @pl.loop(0, tiles)
    def _(i):
        if arrive is not None:
            arrive(i)
        cols = tile(i)
        total = dot(gate_in[...], wg[cols, :], 1, 1) + dot(up_in[...], wu[cols, :], 1, 1)
        held[:, cols] = total.astype(BF16)
        begin(stores(i), sems.at[i])

    finish_tiles(stores, tiles, sems)


def shared_rows(weights, up_in, gate_in):
    span, h = up_in.shape
    width = weights[0].shape[0]
    return call(
        "shared_rows",
        shared_rows_kernel,
        [((span // 4, width), BF16)] * 4,
        [weights[0], weights[1], weights[3], up_in, gate_in],
        [ANY] * 3 + [VMEM] * 2,
        [
            pltpu.VMEM((width, h), BF16),
            pltpu.VMEM((width, h), BF16),
            pltpu.VMEM((span, width), BF16),
            pltpu.SemaphoreType.DMA((width // TILE, 4)),
            pltpu.SemaphoreType.DMA((width // TILE, 4)),
        ],
        2 * 2 * span * width * h,
        [ANY] * 4,
    )


def weight_grads(xv, gv, hidden, up_in, gate_in, outs, held, sems, arrive=None):
    tiles = xv.shape[1] // TILE
    h = outs[2].shape[0]
    hg, hu, hd = held

    def stores(i):
        cols = tile(i)
        pairs = []
        for k in range(len(outs) // 3):
            part = pl.ds(k * h, h)
            pairs += [
                (hg.at[cols, part], outs[3 * k].at[cols, :]),
                (hu.at[cols, part], outs[3 * k + 1].at[cols, :]),
                (hd.at[part, cols], outs[3 * k + 2].at[:, cols]),
            ]
        return pairs

    @pl.loop(0, tiles)
    def _(i):
        if arrive is not None:
            arrive(i)
        cols = tile(i)
        x = xv[:, cols]
        hg[cols, :] = dot(x, gate_in[...], 0, 0).astype(BF16)
        hu[cols, :] = dot(x, up_in[...], 0, 0).astype(BF16)
        hd[:, cols] = dot(hidden[...], gv[:, cols], 0, 0).astype(BF16)
        begin(stores(i), sems.at[i])

    finish_tiles(stores, tiles, sems)


def weight_grad_shapes(width, h):
    return [((width, h), BF16), ((width, h), BF16), ((h, width), BF16)] * 2


def shared_weights_kernel(*refs):
    chunks_x, chunks_g, weights = refs[0:7], refs[7:14], refs[14:18]
    outs, up_in, gate_in = refs[18:24], refs[24], refs[25]
    xv, gv, wg, wu, wd, pg, pu, dh, hidden, hg, hu, hd, sems, out_sems = refs[26:]

    def loads(i):
        cols = tile(i)
        return (
            row_pairs(chunks_x, xv, cols)
            + stacked_pairs(weights, wg, wu, wd, cols, i)
            + row_pairs(chunks_g, gv, cols)
        )

    begin_tiles(loads, xv.shape[1] // TILE, sems)
    a, b, c = forward(xv, gv, wg, wu, wd, pg, pu, dh, lambda i: finish(loads(i), sems.at[i]))
    hidden[...] = a
    up_in[...] = b
    gate_in[...] = c
    weight_grads(xv, gv, hidden, up_in, gate_in, outs, (hg, hu, hd), out_sems)


def shared_weights(chunks_x, chunks_g, weights):
    rows, width = chunks_x[0].shape
    span, h = 4 * rows, 2 * weights[0].shape[1]
    outs = call(
        "shared_weights",
        shared_weights_kernel,
        weight_grad_shapes(width, h // 2) + [((span, h), BF16)] * 2,
        [*chunks_x, *chunks_g, *weights],
        [ANY] * 18,
        [
            pltpu.VMEM((span, width), BF16),
            pltpu.VMEM((span, width), BF16),
            pltpu.VMEM((width, h), BF16),
            pltpu.VMEM((width, h), BF16),
            pltpu.VMEM((h, width), BF16),
            pltpu.VMEM((span, h), F32),
            pltpu.VMEM((span, h), F32),
            pltpu.VMEM((span, h), F32),
            pltpu.VMEM((span, h), BF16),
            pltpu.VMEM((width, h), BF16),
            pltpu.VMEM((width, h), BF16),
            pltpu.VMEM((h, width), BF16),
            pltpu.SemaphoreType.DMA((width // TILE, 19 + 2 * TILE // h)),
            pltpu.SemaphoreType.DMA((width // TILE, 6)),
        ],
        2 * 6 * span * width * h,
        [ANY] * 6 + [VMEM] * 2,
    )
    return outs[:6], outs[6], outs[7]


def routed_rows_kernel(n, *refs):
    inputs, weights, refs = refs[:n], refs[n : n + 6], refs[n + 6 :]
    outs, kept, bundle, refs = refs[:n], refs[n : n + 3], refs[n + 3], refs[n + 4 :]
    xv, gv, wg, wu, wd, pg, pu, dh, hidden, up_in, gate_in, rows, sems, o_sems, k_sems = refs
    width = xv.shape[1]
    tiles = width // TILE
    h = kept[0].shape[1]

    def loads(i):
        pairs = weight_pairs(weights, wg, wu, wd, tile(i))
        gcols = pl.ds(pl.multiple_of(width + i * TILE, TILE), TILE)
        for k, b in enumerate(inputs):
            at = pl.ds(k * b.shape[0], b.shape[0])
            pairs.append((b.at[:, tile(i)], xv.at[at, tile(i)]))
            pairs.append((b.at[:, gcols], gv.at[at, tile(i)]))
        return pairs

    begin_tiles(loads, tiles, sems)
    a, b, c = forward(xv, gv, wg, wu, wd, pg, pu, dh, lambda i: finish(loads(i), sems.at[i]))
    hidden[...] = a
    up_in[...] = b
    gate_in[...] = c
    stores = [(xv, bundle.at[:, pl.ds(0, width)]), (gv, bundle.at[:, pl.ds(width, width)])]
    for k, v in enumerate((hidden, up_in, gate_in)):
        stores.append((v.at[:, pl.ds(0, h)], kept[k]))
        stores.append((v.at[:, pl.ds(h, h)], bundle.at[:, pl.ds(2 * width + k * h, h)]))
    begin(stores, k_sems)
    rows_back(gate_in, up_in, wg, wu, outs, rows, o_sems)
    finish(stores, k_sems)


def routed_rows(tag, inputs, weights):
    width, quarter = weights[0].shape
    h = 2 * quarter
    block = inputs[0].shape[0]
    count = len(inputs)
    span = count * block
    tiles = width // TILE
    outs = [((block, width), BF16)] * count + [((span, quarter), BF16)] * 3
    outs += [((span, 2 * width + 3 * quarter), BF16)]
    outs = call(
        "routed_rows" + tag,
        functools.partial(routed_rows_kernel, count),
        outs,
        [*inputs, *weights],
        [ANY] * (count + 6),
        [
            pltpu.VMEM((span, width), BF16),
            pltpu.VMEM((span, width), BF16),
            pltpu.VMEM((width, h), BF16),
            pltpu.VMEM((width, h), BF16),
            pltpu.VMEM((h, width), BF16),
            pltpu.VMEM((span, h), F32),
            pltpu.VMEM((span, h), F32),
            pltpu.VMEM((span, h), F32),
            pltpu.VMEM((span, h), BF16),
            pltpu.VMEM((span, h), BF16),
            pltpu.VMEM((span, h), BF16),
            pltpu.VMEM((span, width), BF16),
            pltpu.SemaphoreType.DMA((tiles, 6 + 2 * count)),
            pltpu.SemaphoreType.DMA((tiles, count)),
            pltpu.SemaphoreType.DMA((8,)),
        ],
        2 * 5 * span * width * h,
        [ANY] * len(outs),
    )
    return outs[:count], outs[count : count + 3], outs[count + 3]


def routed_weights_kernel(*refs):
    bundles, kept, outs = refs[0:4], (refs[4:7], refs[7:10]), refs[10:13]
    xv, gv, hidden, up_in, gate_in, hg, hu, hd, sems, w_sems, o_sems = refs[13:]
    width = xv.shape[1]
    h = kept[0][0].shape[1]
    inner, at = [], 0
    for i in range(4):
        n = bundles[i].shape[0]
        for k, v in enumerate((hidden, up_in, gate_in)):
            if i < 2:
                source = kept[i][k]
            else:
                source = bundles[i].at[:, pl.ds(2 * width + k * h, h)]
            inner.append((source, v.at[pl.ds(at, n)]))
        at += n

    def loads(i):
        pairs, at = [], 0
        for b in bundles:
            n = b.shape[0]
            gcols = pl.ds(pl.multiple_of(width + i * TILE, TILE), TILE)
            pairs.append((b.at[:, tile(i)], xv.at[pl.ds(at, n), tile(i)]))
            pairs.append((b.at[:, gcols], gv.at[pl.ds(at, n), tile(i)]))
            at += n
        return pairs

    begin(inner, sems)
    begin_tiles(loads, width // TILE, w_sems)
    finish(inner, sems)
    arrive = lambda i: finish(loads(i), w_sems.at[i])
    weight_grads(xv, gv, hidden, up_in, gate_in, outs, (hg, hu, hd), o_sems, arrive)


def routed_weights(own, other, kept, width):
    h = kept[0][0].shape[1]
    span = sum(b.shape[0] for b in (*own, *other))
    tiles = width // TILE
    return call(
        "routed_weights",
        routed_weights_kernel,
        weight_grad_shapes(width, h)[:3],
        [*own, *other, *kept[0], *kept[1]],
        [ANY] * 10,
        [
            pltpu.VMEM((span, width), BF16),
            pltpu.VMEM((span, width), BF16),
            pltpu.VMEM((span, h), BF16),
            pltpu.VMEM((span, h), BF16),
            pltpu.VMEM((span, h), BF16),
            pltpu.VMEM((width, h), BF16),
            pltpu.VMEM((width, h), BF16),
            pltpu.VMEM((h, width), BF16),
            pltpu.SemaphoreType.DMA((12,)),
            pltpu.SemaphoreType.DMA((tiles, 8)),
            pltpu.SemaphoreType.DMA((tiles, 3)),
        ],
        2 * 3 * span * width * h,
        [ANY] * 3,
    )


def grad_pack_kernel(g0, u0, d0, g1, u1, d1, out):
    h = g0.shape[1]
    out[:, 0:h] = (g0[...].astype(F32) + g1[...].astype(F32)).astype(BF16)
    out[:, h : 2 * h] = (u0[...].astype(F32) + u1[...].astype(F32)).astype(BF16)
    for c in range(d0.shape[1] // h):
        cols = slice(c * h, (c + 1) * h)
        block = d0[:, cols].astype(F32) + d1[:, cols].astype(F32)
        out[cols, 2 * h :] = block.astype(BF16)


def grad_pack(own, other):
    width, h = own[0].shape
    return call("grad_pack", grad_pack_kernel, [((width, 3 * h), BF16)], [*own, *other], [VMEM] * 6, [], 3 * width * h)[0]


def grad_sum_kernel(came, out):
    total = came[0].astype(F32)
    for n in range(1, came.shape[0]):
        total = total + came[n].astype(F32)
    total = total.astype(BF16)
    for n in range(came.shape[0]):
        out[n] = total


def grad_sum(came, nodes):
    shape = (nodes, came.shape[0] // nodes, came.shape[1])
    out = call("grad_sum", grad_sum_kernel, [(shape, BF16)], [came.reshape(shape)], [VMEM], [], came.size)[0]
    return out


def grad_unpack_kernel(came, g, u, d):
    h = g.shape[1]
    g[...] = came[:, 0:h]
    u[...] = came[:, h : 2 * h]
    for c in range(d.shape[1] // h):
        d[:, c * h : (c + 1) * h] = came[c * h : (c + 1) * h, 2 * h :]


def grad_unpack(came, width, h):
    outs = [((width, h), BF16), ((width, h), BF16), ((h, width), BF16)]
    return call("grad_unpack", grad_unpack_kernel, outs, [came], [VMEM], [], 3 * width * h)


def add_kernel(a, b, out):
    out[...] = (a[...].astype(F32) + b[...].astype(F32)).astype(BF16)


def add(a, b):
    return call("add", add_kernel, [(a.shape, BF16)], [a, b], [VMEM] * 2, [], a.size)[0]


def return_kernel(b0, b1, b2, b3, out):
    block, width = b0.shape
    part = width // 4
    nodes = block // CAP
    shape = (nodes * RET, block)
    q, i = iota(shape, 0), iota(shape, 1)
    n, j = q >> 3, q & 7
    own = hot((j < CAP) & (i == n * CAP + j))
    other = hot((j >= CAP) & (i == n * CAP + j - CAP))
    for kp in range(4):
        cols = slice(kp * part, (kp + 1) * part)
        out[:, cols] = (
            dot(own, b0[:, cols]) + dot(own, b1[:, cols]) + dot(other, b2[:, cols]) + dot(other, b3[:, cols])
        ).astype(BF16)
    last = None
    for kp in range(4):
        cols = slice(kp * part, (kp + 1) * part)
        get = hot(((j & 3) == kp) & (i == n * CAP + 3 + (j >> 2)))
        term = dot(get, b2[:, cols]) + dot(get, b3[:, cols])
        last = term if last is None else last + term
    out[:, width:] = last.astype(BF16)


def return_pack(blocks):
    block, width = blocks[0].shape
    nodes = block // CAP
    return call(
        "return_pack",
        return_kernel,
        [((nodes * RET, width + width // 4), BF16)],
        blocks,
        [VMEM] * 4,
        [],
        2 * nodes * RET * 4 * block * width,
    )[0]


def combine_kernel(where, meta, back, p0, p1, p2, p3, out):
    rows, width = out.shape
    part = width // 4
    n = back.shape[0]
    row = meta[0:1, :]
    ids = row.astype(I32)
    j = ranks(row) + jnp.where((ids & 1) == where[0] // 2, 0, CAP)
    node = ids >> 1
    c = iota((n, rows), 0)
    head = hot((j < RET) & (c == node * RET + j))
    for kp in range(4):
        cols = slice(kp * part, (kp + 1) * part)
        last = hot((j >= RET) & (c == node * RET + (j - RET) * 4 + kp))
        total = dot(head, back[:, cols], 0, 0) + dot(last, back[:, width:], 0, 0)
        for p in (p0, p1, p2, p3):
            total = total + p[:, cols].astype(F32)
        out[:, cols] = total.astype(BF16)


def combine(where, meta, back, parts):
    rows, width = parts[0].shape
    return call(
        "combine",
        combine_kernel,
        [((rows, width), BF16)],
        [where, meta, back, *parts],
        [SMEM] + [VMEM] * 6,
        [],
        2 * rows * back.shape[0] * width * 2,
    )[0]


def gather_y(v):
    half = v.shape[0] // 2
    v1 = from_y(v, 1)
    v3 = from_y(v, 3)
    top = from_y(v1[:half], 1)
    bottom = from_y(v3[half:], 3)
    return [v, v1, top, bottom, v3]


def on_device(x, g, ids, gate, eg, eu, ed, sg, su, sd):
    rows, width = x.shape
    nodes = lax.axis_size("z") * lax.axis_size("x")
    ny = lax.axis_size("y")
    y = lax.axis_index("y")
    where = y.astype(I32).reshape(1)

    axes = ("z", "x")

    def exchange(v):
        return lax.all_to_all(v, axes, split_axis=0, concat_axis=0, tiled=True)

    half = rows // 2
    def named(name, f, *args):
        with jax.named_scope(name):
            return f(*args)

    def pairs_y(name, v, order):
        return named(name, lambda v: lax.ppermute(v, "y", list(enumerate(order))), v)

    def partner(name, v):
        return pairs_y(name, v, (1, 0, 3, 2))

    def beside(name, v):
        return pairs_y(name, v, (3, 2, 1, 0))

    def across(name, v):
        return pairs_y(name, v, (2, 3, 0, 1))

    top, bottom = slice(0, rows // 2), slice(rows // 2, rows)
    x1t, x3b = named("x1t", from_y, x[top], 1), named("x3b", from_y, x[bottom], 3)
    g1t, g3b = named("g1t", from_y, g[top], 1), named("g3b", from_y, g[bottom], 3)
    x1b, x3t = named("x1b", from_y, x[bottom], 1), named("x3t", from_y, x[top], 3)
    g1b, g3t = named("g1b", from_y, g[bottom], 1), named("g3t", from_y, g[top], 3)
    meta = jnp.concatenate([ids.reshape(1, rows).astype(F32), gate.reshape(1, rows).astype(F32)], 0)
    x2 = [named("xt", from_y, x1t, 1), named("xb", from_y, x3b, 3)]
    g2 = [named("gt", from_y, g1t, 1), named("gb", from_y, g3b, 3)]
    xs, gs = [x, x1t, x1b, *x2, x3t, x3b], [g, g1t, g1b, *g2, g3t, g3b]
    send = pack(where, meta, after(x, x1t, x3b, g1t, g3b), g, nodes)
    msg = named("msg", exchange, send)
    stacked = stack(sg, su, sd)
    shared_w = [sg, su, sd, named("swap_shared", swap_core, stacked)]
    expert_w = []

    grads, up_in, gate_in = shared_weights(xs, gs, shared_w)
    near, far = regroup(after(msg, up_in), nodes, width)
    r1, r2 = partner("r1", near), beside("r2", far)
    r3 = across("r3", after(far, r1, r2))

    swapped = [named("swap_grads", swap_core, v) for v in grads[3:]]
    send = grad_pack(grads[:3], swapped)
    scattered = named("scatter", exchange, send)
    for w in (eg[0], eu[0], ed[0]):
        expert_w += [w, named("swap_expert", swap_core, after(w, send))]

    parts = shared_rows(shared_w, after(up_in, near, send), gate_in)
    (e0, e1, e2), kept0, bundle0 = routed_rows("0", [after(near, parts[0]), r1, r2], expert_w)
    b1, b2 = partner("b1", e1), beside("b2", e2)
    summed = grad_sum(after(scattered, e0), nodes)
    came = named("gather", exchange, summed.reshape(scattered.shape))
    (e3,), kept1, bundle1 = routed_rows("1", [after(r3, summed, b1, b2)], expert_w)
    b3 = across("b3", e3)
    p1, p3 = (named("part", to_y, after(parts[k], e3), k) for k in (1, 3))
    p2 = named("part", to_y, after(parts[2], p1, p3), 2)
    own = [bundle0, bundle1]
    other = [named("swap_bundle", swap_core, b) for b in own]
    e_gate, e_up, e_down = routed_weights(own, other, [kept0, kept1], width)
    send = return_pack([after(e0, came, p1, p3, e_gate), b1, b2, b3])
    returned = named("returned", exchange, after(send, came))
    g_gate, g_up, g_down = grad_unpack(came, width, sg.shape[1])
    out = combine(where, meta, after(returned, g_gate), [parts[0], p1, p2, p3])
    return (out, e_gate[None], e_up[None], e_down[None], g_gate, g_up, g_down)


def solution(mesh):
    whole = Mesh(mesh.devices.reshape(4, 4, 4, 2), ("z", "x", "y", "c"))
    every, local = ("z", "x", "y", "c"), ("y", "c")
    specs = dict(
        rows=P(every, None), expert=P(every, None, None), columns=P(None, local), down=P(local, None)
    )
    return jax.shard_map(
        on_device,
        mesh=whole,
        in_specs=(
            specs["rows"],
            specs["rows"],
            specs["rows"],
            specs["rows"],
            specs["expert"],
            specs["expert"],
            specs["expert"],
            specs["columns"],
            specs["columns"],
            specs["down"],
        ),
        out_specs=(
            specs["rows"],
            specs["expert"],
            specs["expert"],
            specs["expert"],
            specs["columns"],
            specs["columns"],
            specs["down"],
        ),
        check_vma=False,
    )
```

profile of v0, /device:TPU:1, one launch (start us, length us, event | category | flops | bytes accessed | tf_op | source)
XLA Modules:
  0.0 254.9 jit_solution(18171247142369504092)
XLA Ops:
  12.1 7.7 %collective-permute-done.3.refs_13_ = bf16[64,3584]{1,0:T(8,128)(2,1)} collective-permute-done((bf16[64,3584]{1,0:T(8,128)(2,1)S(1)}, bf16[64,3584]{1,0:T(8,128)(2,1)}, u32[]{:S(2)}, u32[]{:S(2)}) %collective-permute-start.3) | collective-permute-done | bytes 458784 | tf_op jit(solution)/shard_map/g3b/ppermute | solution.py:36
  22.5 7.0 %collective-permute-done.1.refs_6_ = bf16[64,3584]{1,0:T(8,128)(2,1)S(1)} collective-permute-done((bf16[64,3584]{1,0:T(8,128)(2,1)S(1)}, bf16[64,3584]{1,0:T(8,128)(2,1)S(1)}, u32[]{:S(2)}, u32[]{:S(2)}) %collective-permute-start.1) | collective-permute-done | bytes 458784 | tf_op jit(solution)/shard_map/x3b/ppermute | solution.py:36
  32.8 6.5 %collective-permute-done.11.refs_12_ = bf16[64,3584]{1,0:T(8,128)(2,1)S(1)} collective-permute-done((bf16[64,3584]{1,0:T(8,128)(2,1)S(1)}, bf16[64,3584]{1,0:T(8,128)(2,1)S(1)}, u32[]{:S(2)}, u32[]{:S(2)}) %collective-permute-start.11) | collective-permute-done | bytes 458784 | tf_op jit(solution)/shard_map/g3t/ppermute | solution.py:36
  42.0 7.1 %collective-permute-done.7.refs_5_ = bf16[64,3584]{1,0:T(8,128)(2,1)S(1)} collective-permute-done((bf16[64,3584]{1,0:T(8,128)(2,1)S(1)}, bf16[64,3584]{1,0:T(8,128)(2,1)S(1)}, u32[]{:S(2)}, u32[]{:S(2)}) %collective-permute-start.7) | collective-permute-done | bytes 458784 | tf_op jit(solution)/shard_map/x3t/ppermute | solution.py:36
  51.9 5.8 %pack.1 = bf16[256,4480]{1,0:T(8,128)(2,1)} custom-call(s32[1]{0:T(128)} %bitcast.where, f32[2,128]{1,0:T(2,128)} %pad_maximum_fusion.meta, bf16[128,3584]{1,0:T(8,128)(2,1)} %refs_0_.1, bf16[128,3584]{1,0:T(8,128)(2,1)} %refs_7_.1), custom_call_target="tpu_custom_call" | custom-call | flops 5637144576 | bytes 33038368 | tf_op jit(solution)/shard_map/pack/pallas_call | solution.py:56
  57.8 7.6 %all-to-all-start = ((bf16[16,16,4480]{2,1,0:T(8,128)(2,1)}), bf16[16,16,4480]{2,1,0:T(8,128)(2,1)S(1)}, u32[]{:S(2)}, u32[]{:S(2)}) async-start(bf16[16,16,4480]{2,1,0:T(8,128)(2,1)} %bitcast.24), calls=%async_computation | async-start | bytes 4587520 | tf_op jit(solution)/shard_map/msg/all_to_all | solution.py:697
  68.9 13.7 %shared_weights.1 = (bf16[3584,128]{1,0:T(8,128)(2,1)}, bf16[3584,128]{1,0:T(8,128)(2,1)}, bf16[128,3584]{1,0:T(8,128)(2,1)}, bf16[3584,128]{1,0:T(8,128)(2,1)},...) custom-call(bf16[128,3584]{1,0:T(8,128)(2,1)} %refs_0_.1, ...), custom_call_target="tpu_custom_call" | custom-call | flops 45097156608 | bytes 150994944 | tf_op jit(solution)/shard_map/shared_weights/pallas_call | solution.py:56
  84.2 8.7 %all-to-all-done = bf16[16,16,4480]{2,1,0:T(8,128)(2,1)S(1)} async-done(((bf16[16,16,4480]{2,1,0:T(8,128)(2,1)}), bf16[16,16,4480]{2,1,0:T(8,128)(2,1)S(1)}, u32[]{:S(2)}, u32[]{:S(2)}) %all-to-all-start) | async-done | bytes 2293792 | tf_op jit(solution)/shard_map/msg/all_to_all | solution.py:697
  94.3 4.2 %regroup.1 = (bf16[80,7168]{1,0:T(8,128)(2,1)}, bf16[80,7168]{1,0:T(8,128)(2,1)}) custom-call(bf16[256,4480]{1,0:T(8,128)(2,1)} %bitcast.23), custom_call_target="tpu_custom_call" | custom-call | flops 734003200 | bytes 4587520 | tf_op jit(solution)/shard_map/regroup/pallas_call | solution.py:56
  103.3 4.8 %grad_pack.1 = bf16[3584,384]{1,0:T(8,128)(2,1)} custom-call(bf16[3584,128]{1,0:T(8,128)(2,1)} %get-tuple-element.59.g0, bf16[3584,128]{1,0:T(8,128)(2,1)} %get-tuple-element.60.u0, bf16[128,3584]{1,0:T(8,128)(2,1)} %get-tuple-element.61.d0, bf16[3584,128]{1,0:T(8,128)(2,1)} %copy-done.6, bf16[3584,128]{1,0:T(8,128)(2,1)} %collective-permute-done.14.u1, ...), custom_call_target="tpu_custom_call" | custom-call | flops 1376256 | bytes 8257536 | tf_op jit(solution)/shard_map/grad_pack/pallas_call | solution.py:56
  108.1 4.2 %collective-permute-start.18 = (bf16[3584,256]{1,0:T(8,128)(2,1)}, bf16[3584,256]{1,0:T(8,128)(2,1)}, u32[]{:S(2)}, u32[]{:S(2)}) collective-permute-start(bf16[3584,256]{1,0:T(8,128)(2,1)} %bitcast.5.refs_3_.refs_1_), channel_id=1, source_target_pairs={{0,1},{1,0},{2,3},{3,2},{4,5},{5,4},{6,7},{7,6},{8,9},{9,8},{10,11... | collective-permute-start | bytes 5505032 | tf_op jit(solution)/shard_map/swap_expert/ppermute | solution.py:45
  116.6 6.7 %shared_rows.1 = (bf16[128,3584]{1,0:T(8,128)(2,1)}, bf16[128,3584]{1,0:T(8,128)(2,1)}, bf16[128,3584]{1,0:T(8,128)(2,1)}, bf16[128,3584]{1,0:T(8,128)(2,1)}) custom-call(bf16[3584,128]{1,0:T(8,128)(2,1)} %go.1, bf16[3584,128]{1,0:T(8,128)(2,1)} %uo.1, bf16[3584,384]{1,0:T(8,128)(2,1)} %collective-permute-done.12.refs_17_.came, ...), custom_call_target="tpu_custom_call" | custom-call | flops 37580963840 | bytes 175636480 | tf_op jit(solution)/shard_map/shared_rows/pallas_call | solution.py:56
  125.5 11.0 %routed_rows0.1 = (bf16[80,3584]{1,0:T(8,128)(2,1)}, bf16[80,3584]{1,0:T(8,128)(2,1)}, bf16[80,3584]{1,0:T(8,128)(2,1)}, bf16[240,256]{1,0:T(8,128)(2,1)}, bf16[...) custom-call(bf16[80,7168]{1,0:T(8,128)(2,1)} %get-tuple-element.68.refs_0_, ...), custom_call_target="tpu_custom_call" | custom-call | flops 17616076800 | bytes 81395712 | tf_op jit(solution)/shard_map/routed_rows0/pallas_call | solution.py:56
  139.4 5.7 %collective-permute-start.26 = (bf16[240,7936]{1,0:T(8,128)(2,1)}, bf16[240,7936]{1,0:T(8,128)(2,1)}, u32[]{:S(2)}, u32[]{:S(2)}) collective-permute-start(bf16[240,7936]{1,0:T(8,128)(2,1)} %get-tuple-element.84.refs_0_), channel_id=1, source_target_pairs={{0,1},{1,0},{2,3},{3,2},{4,5},{5,4},{6,7},{7,6},{8,9},{9,8},{10,11... | collective-permute-start | bytes 11427848 | tf_op jit(solution)/shard_map/swap_bundle/ppermute | solution.py:45
  145.2 14.9 %all-to-all-done.1 = bf16[16,224,384]{2,1,0:T(8,128)(2,1)S(1)} async-done(((bf16[16,224,384]{2,1,0:T(8,128)(2,1)}), bf16[16,224,384]{2,1,0:T(8,128)(2,1)S(1)}, u32[]{:S(2)}, u32[]{:S(2)}) %all-to-all-start.1) | async-done | bytes 2752544 | tf_op jit(solution)/shard_map/scatter/all_to_all | solution.py:697
  169.4 9.6 %routed_rows1.1 = (bf16[80,3584]{1,0:T(8,128)(2,1)}, bf16[80,256]{1,0:T(8,128)(2,1)}, bf16[80,256]{1,0:T(8,128)(2,1)}, bf16[80,256]{1,0:T(8,128)(2,1)}, bf16[80,7936]{1,0:T(8,128)(2,1)}) custom-call(bf16[80,7168]{1,0:T(8,128)(2,1)} %collective-permute-done.21.refs_0_, bf16[3584,256]{1,0:T(8,128)(2,1)} %bitcast.5.refs_3_.refs_1_, ...), custom_call_target="tpu_custom_call" | custom-call | flops 29360128000 | bytes 282460160 | tf_op jit(solution)/shard_map/routed_rows1/pallas_call | solution.py:56
  183.5 8.9 %routed_weights.1 = (bf16[3584,256]{1,0:T(8,128)(2,1)}, bf16[3584,256]{1,0:T(8,128)(2,1)}, bf16[256,3584]{1,0:T(8,128)(2,1)}) custom-call(bf16[240,7936]{1,0:T(8,128)(2,1)} %get-tuple-element.84.refs_0_, bf16[80,7936]{1,0:T(8,128)(2,1)} %get-tuple-element.85.refs_1_, bf16[240,7936]{1,0:T(8,128)(2,1)} %collective-permute-done.26.refs_2_, ...), custom_call_target="tpu_custom_call" | custom-call | flops 7046430720 | bytes 32309248 | tf_op jit(solution)/shard_map/routed_weights/pallas_call | solution.py:56
  192.4 10.0 %collective-permute-done.25.p3 = bf16[128,3584]{1,0:T(8,128)(2,1)} collective-permute-done((bf16[128,3584]{1,0:T(8,128)(2,1)}, bf16[128,3584]{1,0:T(8,128)(2,1)}, u32[]{:S(2)}, u32[]{:S(2)}) %collective-permute-start.25) | collective-permute-done | bytes 917536 | tf_op jit(solution)/shard_map/part/ppermute | solution.py:41
  204.7 5.1 %all-to-all-done.2 = bf16[16,224,384]{2,1,0:T(8,128)(2,1)S(1)} async-done(((bf16[16,224,384]{2,1,0:T(8,128)(2,1)}), bf16[16,224,384]{2,1,0:T(8,128)(2,1)S(1)}, u32[]{:S(2)}, u32[]{:S(2)}) %all-to-all-start.2) | async-done | bytes 2752544 | tf_op jit(solution)/shard_map/gather/all_to_all | solution.py:697
  209.8 6.4 %collective-permute-done.28.b3 = bf16[80,3584]{1,0:T(8,128)(2,1)S(1)} collective-permute-done((bf16[80,3584]{1,0:T(8,128)(2,1)}, bf16[80,3584]{1,0:T(8,128)(2,1)S(1)}, u32[]{:S(2)}, u32[]{:S(2)}) %collective-permute-start.28) | collective-permute-done | bytes 573472 | tf_op jit(solution)/shard_map/b3/ppermute | solution.py:705
  221.2 7.0 %all-to-all-start.3 = ((bf16[16,8,4480]{2,1,0:T(8,128)(2,1)}), bf16[16,8,4480]{2,1,0:T(8,128)(2,1)}, u32[]{:S(2)}, u32[]{:S(2)}) async-start(bf16[16,8,4480]{2,1,0:T(8,128)(2,1)} %bitcast.22), calls=%async_computation.3 | async-start | bytes 2293760 | tf_op jit(solution)/shard_map/returned/all_to_all | solution.py:697
  233.1 11.1 %all-to-all-done.3 = bf16[16,8,4480]{2,1,0:T(8,128)(2,1)} async-done(((bf16[16,8,4480]{2,1,0:T(8,128)(2,1)}), bf16[16,8,4480]{2,1,0:T(8,128)(2,1)}, u32[]{:S(2)}, u32[]{:S(2)}) %all-to-all-start.3) | async-done | bytes 1146912 | tf_op jit(solution)/shard_map/returned/all_to_all | solution.py:697
  244.1 5.4 %collective-permute-done.29.p2 = bf16[128,3584]{1,0:T(8,128)(2,1)S(1)} collective-permute-done((bf16[128,3584]{1,0:T(8,128)(2,1)}, bf16[128,3584]{1,0:T(8,128)(2,1)S(1)}, u32[]{:S(2)}, u32[]{:S(2)}) %collective-permute-start.29) | collective-permute-done | bytes 917536 | tf_op jit(solution)/shard_map/part/ppermute | solution.py:41
  250.6 4.3 %combine.1 = bf16[128,3584]{1,0:T(8,128)(2,1)} custom-call(s32[1]{0:T(128)} %bitcast.where, f32[2,128]{1,0:T(2,128)} %pad_maximum_fusion.meta, bf16[128,4480]{1,0:T(8,128)(2,1)} %bitcast.13.back, bf16[128,3584]{1,0:T(8,128)(2,1)} %get-tuple-element.67.p0, bf16[128,3584]{1,0:T(8,128)(2,1)} %collective-permute-done.24.p1, bf16[128,3584]{1,0:T(8,128)(2,1)} %copy-done.3, ...), custom_call_target="tpu_custom_call" | custom-call | flops 234881024 | bytes 5735428 | tf_op jit(solution)/shard_map/combine/pallas_call | solution.py:56
  (96 shorter events, 70.4 us)
Async XLA Ops:
  4.6 64.4 %collective-permute-start.12 = (bf16[3584,384]{1,0:T(8,128)(2,1)}, bf16[3584,384]{1,0:T(8,128)(2,1)}, u32[]{:S(2)}, u32[]{:S(2)}) collective-permute-start(bf16[3584,384]{1,0:T(8,128)(2,1)} %stack.1), channel_id=1, source_target_pairs={{0,1},{1,0},{2,3},{3,2},{4,5},{5,4},{6,7},{7,6},{8,9},{9,8},{10,11... | collective-permute-start | bytes 8257544 | tf_op jit(solution)/shard_map/swap_shared/ppermute | solution.py:45
  9.4 20.1 %collective-permute-start.1 = (bf16[64,3584]{1,0:T(8,128)(2,1)S(1)}, bf16[64,3584]{1,0:T(8,128)(2,1)S(1)}, u32[]{:S(2)}, u32[]{:S(2)}) collective-permute-start(bf16[64,3584]{1,0:T(8,128)(2,1)S(1)} %get-tuple-element.105), channel_id=1, source_target_pairs={{0,2},{2,4},{4,6},{6,0},{1,3},{3,5},{5,7},{7,1},{8,10},{10,12},{12... | collective-permute-start | bytes 1376264 | tf_op jit(solution)/shard_map/x3b/ppermute | solution.py:36
  9.4 20.1 %collective-permute-start.2 = (bf16[64,3584]{1,0:T(8,128)(2,1)S(1)}, bf16[64,3584]{1,0:T(8,128)(2,1)}, u32[]{:S(2)}, u32[]{:S(2)}) collective-permute-start(bf16[64,3584]{1,0:T(8,128)(2,1)S(1)} %get-tuple-element.104), channel_id=1, source_target_pairs={{0,6},{2,0},{4,2},{6,4},{1,7},{3,1},{5,3},{7,5},{8,14},{10,8},{12,... | collective-permute-start | bytes 1376264 | tf_op jit(solution)/shard_map/g1t/ppermute | solution.py:36
  29.5 19.7 %collective-permute-start.7 = (bf16[64,3584]{1,0:T(8,128)(2,1)S(1)}, bf16[64,3584]{1,0:T(8,128)(2,1)S(1)}, u32[]{:S(2)}, u32[]{:S(2)}) collective-permute-start(bf16[64,3584]{1,0:T(8,128)(2,1)S(1)} %get-tuple-element.106), channel_id=1, source_target_pairs={{0,2},{2,4},{4,6},{6,0},{1,3},{3,5},{5,7},{7,1},{8,10},{10,12},{12... | collective-permute-start | bytes 1376264 | tf_op jit(solution)/shard_map/x3t/ppermute | solution.py:36
  29.6 19.6 %collective-permute-start.8 = (bf16[64,3584]{1,0:T(8,128)(2,1)S(1)}, bf16[64,3584]{1,0:T(8,128)(2,1)S(1)}, u32[]{:S(2)}, u32[]{:S(2)}) collective-permute-start(bf16[64,3584]{1,0:T(8,128)(2,1)S(1)} %get-tuple-element.103), channel_id=1, source_target_pairs={{0,6},{2,0},{4,2},{6,4},{1,7},{3,1},{5,3},{7,5},{8,14},{10,8},{12,... | collective-permute-start | bytes 1376264 | tf_op jit(solution)/shard_map/g1b/ppermute | solution.py:36
  39.3 26.1 %collective-permute-start.10 = (bf16[64,3584]{1,0:T(8,128)(2,1)}, bf16[64,3584]{1,0:T(8,128)(2,1)}, u32[]{:S(2)}, u32[]{:S(2)}) collective-permute-start(bf16[64,3584]{1,0:T(8,128)(2,1)} %collective-permute-done.3.refs_13_), channel_id=1, source_target_pairs={{0,2},{2,4},{4,6},{6,0},{1,3},{3,5},{5,7},{7,1},{8,10},{10,12},{12... | collective-permute-start | bytes 1376264 | tf_op jit(solution)/shard_map/gb/ppermute | solution.py:36
  39.4 26.1 %collective-permute-start.5 = (bf16[64,3584]{1,0:T(8,128)(2,1)S(1)}, bf16[64,3584]{1,0:T(8,128)(2,1)}, u32[]{:S(2)}, u32[]{:S(2)}) collective-permute-start(bf16[64,3584]{1,0:T(8,128)(2,1)S(1)} %collective-permute-done.refs_1_), channel_id=1, source_target_pairs={{0,6},{2,0},{4,2},{6,4},{1,7},{3,1},{5,3},{7,5},{8,14},{10,8},{12,... | collective-permute-start | bytes 1376264 | tf_op jit(solution)/shard_map/xt/ppermute | solution.py:36
  49.2 19.8 %collective-permute-start.6 = (bf16[64,3584]{1,0:T(8,128)(2,1)S(1)}, bf16[64,3584]{1,0:T(8,128)(2,1)}, u32[]{:S(2)}, u32[]{:S(2)}) collective-permute-start(bf16[64,3584]{1,0:T(8,128)(2,1)S(1)} %collective-permute-done.1.refs_6_), channel_id=1, source_target_pairs={{0,2},{2,4},{4,6},{6,0},{1,3},{3,5},{5,7},{7,1},{8,10},{10,12},{12... | collective-permute-start | bytes 1376264 | tf_op jit(solution)/shard_map/xb/ppermute | solution.py:36
  49.2 19.7 %collective-permute-start.9 = (bf16[64,3584]{1,0:T(8,128)(2,1)}, bf16[64,3584]{1,0:T(8,128)(2,1)}, u32[]{:S(2)}, u32[]{:S(2)}) collective-permute-start(bf16[64,3584]{1,0:T(8,128)(2,1)} %collective-permute-done.2.refs_8_), channel_id=1, source_target_pairs={{0,6},{2,0},{4,2},{6,4},{1,7},{3,1},{5,3},{7,5},{8,14},{10,8},{12,... | collective-permute-start | bytes 1376264 | tf_op jit(solution)/shard_map/gt/ppermute | solution.py:36
  57.8 35.0 %all-to-all-start = ((bf16[16,16,4480]{2,1,0:T(8,128)(2,1)}), bf16[16,16,4480]{2,1,0:T(8,128)(2,1)S(1)}, u32[]{:S(2)}, u32[]{:S(2)}) async-start(bf16[16,16,4480]{2,1,0:T(8,128)(2,1)} %bitcast.24), calls=%async_computation | async-start | bytes 4587520 | tf_op jit(solution)/shard_map/msg/all_to_all | solution.py:697
  82.7 19.7 %collective-permute-start.13 = (bf16[3584,128]{1,0:T(8,128)(2,1)}, bf16[3584,128]{1,0:T(8,128)(2,1)S(1)}, u32[]{:S(2)}, u32[]{:S(2)}) collective-permute-start(bf16[3584,128]{1,0:T(8,128)(2,1)} %get-tuple-element.62), channel_id=1, source_target_pairs={{0,1},{1,0},{2,3},{3,2},{4,5},{5,4},{6,7},{7,6},{8,9},{9,8},{10,11... | collective-permute-start | bytes 2752520 | tf_op jit(solution)/shard_map/swap_grads/ppermute | solution.py:45
  98.5 24.9 %collective-permute-start.16 = (bf16[80,7168]{1,0:T(8,128)(2,1)}, bf16[80,7168]{1,0:T(8,128)(2,1)}, u32[]{:S(2)}, u32[]{:S(2)}) collective-permute-start(bf16[80,7168]{1,0:T(8,128)(2,1)} %get-tuple-element.68.refs_0_), channel_id=1, source_target_pairs={{0,2},{2,0},{4,6},{6,4},{1,3},{3,1},{5,7},{7,5},{8,10},{10,8},{12,... | collective-permute-start | bytes 3440648 | tf_op jit(solution)/shard_map/r1/ppermute | solution.py:705
  100.8 24.3 %collective-permute-start.17 = (bf16[80,7168]{1,0:T(8,128)(2,1)}, bf16[80,7168]{1,0:T(8,128)(2,1)}, u32[]{:S(2)}, u32[]{:S(2)}) collective-permute-start(bf16[80,7168]{1,0:T(8,128)(2,1)} %get-tuple-element.76), channel_id=1, source_target_pairs={{0,6},{2,4},{4,2},{6,0},{1,7},{3,5},{5,3},{7,1},{8,14},{10,12},{12... | collective-permute-start | bytes 3440648 | tf_op jit(solution)/shard_map/r2/ppermute | solution.py:705
  112.9 47.3 %all-to-all-start.1 = ((bf16[16,224,384]{2,1,0:T(8,128)(2,1)}), bf16[16,224,384]{2,1,0:T(8,128)(2,1)S(1)}, u32[]{:S(2)}, u32[]{:S(2)}) async-start(bf16[16,224,384]{2,1,0:T(8,128)(2,1)} %bitcast.21), calls=%async_computation.1 | async-start | bytes 5505024 | tf_op jit(solution)/shard_map/scatter/all_to_all | solution.py:697
  125.1 44.2 %collective-permute-start.21 = (bf16[80,7168]{1,0:T(8,128)(2,1)}, bf16[80,7168]{1,0:T(8,128)(2,1)}, u32[]{:S(2)}, u32[]{:S(2)}) collective-permute-start(bf16[80,7168]{1,0:T(8,128)(2,1)} %get-tuple-element.76), channel_id=1, source_target_pairs={{0,4},{2,6},{4,0},{6,2},{1,5},{3,7},{5,1},{7,3},{8,12},{10,14},{12... | collective-permute-start | bytes 3440648 | tf_op jit(solution)/shard_map/r3/ppermute | solution.py:705
  136.5 32.8 %collective-permute-start.22 = (bf16[80,3584]{1,0:T(8,128)(2,1)}, bf16[80,3584]{1,0:T(8,128)(2,1)S(1)}, u32[]{:S(2)}, u32[]{:S(2)}) collective-permute-start(bf16[80,3584]{1,0:T(8,128)(2,1)} %get-tuple-element.77), channel_id=1, source_target_pairs={{0,2},{2,0},{4,6},{6,4},{1,3},{3,1},{5,7},{7,5},{8,10},{10,8},{12,... | collective-permute-start | bytes 1720328 | tf_op jit(solution)/shard_map/b1/ppermute | solution.py:705
  138.4 31.0 %collective-permute-start.23 = (bf16[80,3584]{1,0:T(8,128)(2,1)}, bf16[80,3584]{1,0:T(8,128)(2,1)}, u32[]{:S(2)}, u32[]{:S(2)}) collective-permute-start(bf16[80,3584]{1,0:T(8,128)(2,1)} %get-tuple-element.78), channel_id=1, source_target_pairs={{0,6},{2,4},{4,2},{6,0},{1,7},{3,5},{5,3},{7,1},{8,14},{10,12},{12... | collective-permute-start | bytes 1720328 | tf_op jit(solution)/shard_map/b2/ppermute | solution.py:705
  139.4 44.1 %collective-permute-start.26 = (bf16[240,7936]{1,0:T(8,128)(2,1)}, bf16[240,7936]{1,0:T(8,128)(2,1)}, u32[]{:S(2)}, u32[]{:S(2)}) collective-permute-start(bf16[240,7936]{1,0:T(8,128)(2,1)} %get-tuple-element.84.refs_0_), channel_id=1, source_target_pairs={{0,1},{1,0},{2,3},{3,2},{4,5},{5,4},{6,7},{7,6},{8,9},{9,8},{10,11... | collective-permute-start | bytes 11427848 | tf_op jit(solution)/shard_map/swap_bundle/ppermute | solution.py:45
  165.3 44.5 %all-to-all-start.2 = ((bf16[16,224,384]{2,1,0:T(8,128)(2,1)}), bf16[16,224,384]{2,1,0:T(8,128)(2,1)S(1)}, u32[]{:S(2)}, u32[]{:S(2)}) async-start(bf16[16,224,384]{2,1,0:T(8,128)(2,1)} %grad_sum.1), calls=%async_computation.2 | async-start | bytes 5505024 | tf_op jit(solution)/shard_map/gather/all_to_all | solution.py:697
  180.1 22.2 %collective-permute-start.25 = (bf16[128,3584]{1,0:T(8,128)(2,1)}, bf16[128,3584]{1,0:T(8,128)(2,1)}, u32[]{:S(2)}, u32[]{:S(2)}) collective-permute-start(bf16[128,3584]{1,0:T(8,128)(2,1)} %get-tuple-element.83), channel_id=1, source_target_pairs={{0,6},{2,0},{4,2},{6,4},{1,7},{3,1},{5,3},{7,5},{8,14},{10,8},{12,... | collective-permute-start | bytes 2752520 | tf_op jit(solution)/shard_map/part/ppermute | solution.py:41
  181.2 23.5 %collective-permute-start.24 = (bf16[128,3584]{1,0:T(8,128)(2,1)}, bf16[128,3584]{1,0:T(8,128)(2,1)}, u32[]{:S(2)}, u32[]{:S(2)}) collective-permute-start(bf16[128,3584]{1,0:T(8,128)(2,1)} %get-tuple-element.81), channel_id=1, source_target_pairs={{0,2},{2,4},{4,6},{6,0},{1,3},{3,5},{5,7},{7,1},{8,10},{10,12},{12... | collective-permute-start | bytes 2752520 | tf_op jit(solution)/shard_map/part/ppermute | solution.py:41
  181.6 34.6 %collective-permute-start.28 = (bf16[80,3584]{1,0:T(8,128)(2,1)}, bf16[80,3584]{1,0:T(8,128)(2,1)S(1)}, u32[]{:S(2)}, u32[]{:S(2)}) collective-permute-start(bf16[80,3584]{1,0:T(8,128)(2,1)} %get-tuple-element.80), channel_id=1, source_target_pairs={{0,4},{2,6},{4,0},{6,2},{1,5},{3,7},{5,1},{7,3},{8,12},{10,14},{12... | collective-permute-start | bytes 1720328 | tf_op jit(solution)/shard_map/b3/ppermute | solution.py:705
  221.2 22.9 %all-to-all-start.3 = ((bf16[16,8,4480]{2,1,0:T(8,128)(2,1)}), bf16[16,8,4480]{2,1,0:T(8,128)(2,1)}, u32[]{:S(2)}, u32[]{:S(2)}) async-start(bf16[16,8,4480]{2,1,0:T(8,128)(2,1)} %bitcast.22), calls=%async_computation.3 | async-start | bytes 2293760 | tf_op jit(solution)/shard_map/returned/all_to_all | solution.py:697
  228.2 21.4 %collective-permute-start.29 = (bf16[128,3584]{1,0:T(8,128)(2,1)}, bf16[128,3584]{1,0:T(8,128)(2,1)S(1)}, u32[]{:S(2)}, u32[]{:S(2)}) collective-permute-start(bf16[128,3584]{1,0:T(8,128)(2,1)} %get-tuple-element.98), channel_id=1, source_target_pairs={{0,4},{2,6},{4,0},{6,2},{1,5},{3,7},{5,1},{7,3},{8,12},{10,14},{12... | collective-permute-start | bytes 2752520 | tf_op jit(solution)/shard_map/part/ppermute | solution.py:41
  (27 other events, 341.0 us)
where the time goes:
time: 257 us; the launch traced here: 255 us
  waiting for transfers between devices  97.6 us (38%)
  Pallas kernels  84.6 us (33%)
  starting transfers between devices  65.3 us (25%)
  local copies, waits for them, and re-layouts  5.84 us (2%)
    pallas_call x13, Pallas kernels, call(): pl.pallas_call(body, out_shape=out_shape, in_specs=specs, out_specs=out_s...  84.6 us
    all_to_all x4, waiting for transfers between devices, exchange(): return lax.all_to_all(v, axes, split_axis=0, concat_axis=0, tiled=True)  39.8 us
    ppermute x12, waiting for transfers between devices, from_y(): return lax.ppermute(v, 'y', [(i, (i - k) % n) for i in range(n)])  31.9 us
    all_to_all x4, starting transfers between devices, exchange(): return lax.all_to_all(v, axes, split_axis=0, concat_axis=0, tiled=True)  22.3 us
    ppermute x3, waiting for transfers between devices, to_y(): return lax.ppermute(v, 'y', [(i, (i + k) % n) for i in range(n)])  17.7 us
    ppermute x12, starting transfers between devices, from_y(): return lax.ppermute(v, 'y', [(i, (i - k) % n) for i in range(n)])  16.7 us
    ppermute x9, starting transfers between devices, swap_core(): return lax.ppermute(v, 'c', [(0, 1), (1, 0)])  14.5 us
    ppermute x6, starting transfers between devices, pairs_y(): lax.ppermute(v, 'y', list(enumerate(order)))  9.13 us
  transfers between devices with their start and end apart: 34, of which 14 were waited for; matrix products, arithmetic and copies ran while one was open for 0% of the time, Pallas kernels for 28%

commit v1 on v0

--- a/solution.py
+++ b/solution.py
@@ -10,7 +10,7 @@
 CAP = 5
 RET = 8
 TILE = 512
-WEIGHT = {'pack': 8, 'shared_weights': 8, 'routed_rows0': 4, 'routed_rows1': 20, 'routed_weights': 2, 'shared_rows': 20}
+WEIGHT = {'pack': 8, 'shared_weights': 8, 'routed_rows0': .05, 'routed_rows1': 20, 'routed_weights': .05, 'shared_rows': 20, 'regroup': .05, 'grad_pack': .05, 'return_pack': .05, 'combine': .05, 'grad_unpack': .05}
 F32 = jnp.float32
 BF16 = jnp.bfloat16
 I32 = jnp.int32
@@ -719,42 +719,41 @@
     x1b, x3t = named("x1b", from_y, x[bottom], 1), named("x3t", from_y, x[top], 3)
     g1b, g3t = named("g1b", from_y, g[bottom], 1), named("g3t", from_y, g[top], 3)
     meta = jnp.concatenate([ids.reshape(1, rows).astype(F32), gate.reshape(1, rows).astype(F32)], 0)
-    x2 = [named("xt", from_y, x1t, 1), named("xb", from_y, x3b, 3)]
-    g2 = [named("gt", from_y, g1t, 1), named("gb", from_y, g3b, 3)]
+    send = pack(where, meta, after(x, x1t, x3b, g1t, g3b), g, nodes)
+    x2 = [named("xt", from_y, after(x1t, send), 1), named("xb", from_y, after(x3b, send), 3)]
+    g2 = [named("gt", from_y, after(g1t, send), 1), named("gb", from_y, after(g3b, send), 3)]
     xs, gs = [x, x1t, x1b, *x2, x3t, x3b], [g, g1t, g1b, *g2, g3t, g3b]
-    send = pack(where, meta, after(x, x1t, x3b, g1t, g3b), g, nodes)
     msg = named("msg", exchange, send)
     stacked = stack(sg, su, sd)
     shared_w = [sg, su, sd, named("swap_shared", swap_core, stacked)]
     expert_w = []
 
     grads, up_in, gate_in = shared_weights(xs, gs, shared_w)
-    near, far = regroup(after(msg, up_in), nodes, width)
-    r1, r2 = partner("r1", near), beside("r2", far)
+    swapped = [named("swap_grads", swap_core, v) for v in grads[3:]]
+    for w in (eg[0], eu[0], ed[0]):
+        expert_w += [w, named("swap_expert", swap_core, after(w, xs[3]))]
+    parts = shared_rows(shared_w, after(up_in, *expert_w[1::2]), gate_in)
+    p1, p3 = (named("part", to_y, parts[k], k) for k in (1, 3))
+    send = grad_pack([after(grads[0], parts[0]), *grads[1:3]], swapped)
+    scattered = named("scatter", exchange, after(send, msg))
+
+    near, far = regroup(after(msg, send), nodes, width)
+    r1, r2 = partner("r1", after(near, p1, p3)), beside("r2", after(far, p1, p3))
     r3 = across("r3", after(far, r1, r2))
-
-    swapped = [named("swap_grads", swap_core, v) for v in grads[3:]]
-    send = grad_pack(grads[:3], swapped)
-    scattered = named("scatter", exchange, send)
-    for w in (eg[0], eu[0], ed[0]):
-        expert_w += [w, named("swap_expert", swap_core, after(w, send))]
-
-    parts = shared_rows(shared_w, after(up_in, near, send), gate_in)
-    (e0, e1, e2), kept0, bundle0 = routed_rows("0", [after(near, parts[0]), r1, r2], expert_w)
+    (e0, e1, e2), kept0, bundle0 = routed_rows("0", [near, r1, r2], expert_w)
     b1, b2 = partner("b1", e1), beside("b2", e2)
     summed = grad_sum(after(scattered, e0), nodes)
     came = named("gather", exchange, summed.reshape(scattered.shape))
-    (e3,), kept1, bundle1 = routed_rows("1", [after(r3, summed, b1, b2)], expert_w)
+    (e3,), kept1, bundle1 = routed_rows("1", [after(r3, summed)], expert_w)
     b3 = across("b3", e3)
-    p1, p3 = (named("part", to_y, after(parts[k], e3), k) for k in (1, 3))
-    p2 = named("part", to_y, after(parts[2], p1, p3), 2)
+    p2 = named("part", to_y, after(parts[2], e3), 2)
+    send = return_pack([after(e0, came), b1, b2, b3])
+    returned = named("returned", exchange, after(send, came))
     own = [bundle0, bundle1]
-    other = [named("swap_bundle", swap_core, b) for b in own]
+    other = [named("swap_bundle", swap_core, after(b, send)) for b in own]
     e_gate, e_up, e_down = routed_weights(own, other, [kept0, kept1], width)
-    send = return_pack([after(e0, came, p1, p3, e_gate), b1, b2, b3])
-    returned = named("returned", exchange, after(send, came))
     g_gate, g_up, g_down = grad_unpack(came, width, sg.shape[1])
-    out = combine(where, meta, after(returned, g_gate), [parts[0], p1, p2, p3])
+    out = combine(where, meta, after(returned, g_gate, e_gate), [parts[0], p1, p2, p3])
     return (out, e_gate[None], e_up[None], e_down[None], g_gate, g_up, g_down)
 
 

time: 257 us -> 247 us (0.961)
  waiting for transfers between devices: 97.6 us -> 84 us
  starting transfers between devices: 65.3 us -> 68.5 us
    ppermute x6, waiting for transfers between devices: 8.12 us -> 25.6 us  [pairs_y(): lax.ppermute(v, 'y', list(enumerate(order)))]
    all_to_all x4, waiting for transfers between devices: 39.8 us -> 26.5 us  [exchange(): return lax.all_to_all(v, axes, split_axis=0, concat_axis=0, tiled=True)]
    ppermute x3, waiting for transfers between devices: 17.7 us -> 7 us  [to_y(): return lax.ppermute(v, 'y', [(i, (i + k) % n) for i in range(n)])]
    ppermute x12, waiting for transfers between devices: 31.9 us -> 24.9 us  [from_y(): return lax.ppermute(v, 'y', [(i, (i - k) % n) for i in range(n)])]
    all_to_all x4, starting transfers between devices: 22.3 us -> 27.1 us  [exchange(): return lax.all_to_all(v, axes, split_axis=0, concat_axis=0, tiled=True)]
    ppermute x6, starting transfers between devices: 9.13 us -> 6.47 us  [pairs_y(): lax.ppermute(v, 'y', list(enumerate(order)))]
    unnamed x34 -> x30, local copies, waits for them, and re-layouts: 5.72 us -> 5.67 us
  transfers between devices with their start and end apart: 34 -> 34, of which waited for: 14 -> 11; matrix products, arithmetic and copies ran while one was open for 0% -> 1% of each run, Pallas kernels for 28% -> 31%
where the time goes in v1:
time: 247 us; the launch traced here: 246 us
  Pallas kernels  84.6 us (34%)
  waiting for transfers between devices  84 us (34%)
  starting transfers between devices  68.5 us (28%)
  local copies, waits for them, and re-layouts  7.72 us (3%)
    pallas_call x13, Pallas kernels, call(): pl.pallas_call(body, out_shape=out_shape, in_specs=specs, out_specs=out_s...  84.6 us
    all_to_all x4, starting transfers between devices, exchange(): return lax.all_to_all(v, axes, split_axis=0, concat_axis=0, tiled=True)  27.1 us
    all_to_all x4, waiting for transfers between devices, exchange(): return lax.all_to_all(v, axes, split_axis=0, concat_axis=0, tiled=True)  26.5 us
    ppermute x6, waiting for transfers between devices, pairs_y(): lax.ppermute(v, 'y', list(enumerate(order)))  25.6 us
    ppermute x12, waiting for transfers between devices, from_y(): return lax.ppermute(v, 'y', [(i, (i - k) % n) for i in range(n)])  24.9 us
    ppermute x12, starting transfers between devices, from_y(): return lax.ppermute(v, 'y', [(i, (i - k) % n) for i in range(n)])  17.1 us
    ppermute x9, starting transfers between devices, swap_core(): return lax.ppermute(v, 'c', [(0, 1), (1, 0)])  14 us
    ppermute x3, waiting for transfers between devices, to_y(): return lax.ppermute(v, 'y', [(i, (i + k) % n) for i in range(n)])  7 us
  transfers between devices with their start and end apart: 34, of which 11 were waited for; matrix products, arithmetic and copies ran while one was open for 1% of the time, Pallas kernels for 31%

profile of v1, /device:TPU:1, one launch (start us, length us, event | category | flops | bytes accessed | tf_op | source)
XLA Modules:
  0.0 246.3 jit_solution(1957479841879665459)
XLA Ops:
  17.2 8.3 %collective-permute-done.3.refs_13_ = bf16[64,3584]{1,0:T(8,128)(2,1)S(1)} collective-permute-done((bf16[64,3584]{1,0:T(8,128)(2,1)S(1)}, bf16[64,3584]{1,0:T(8,128)(2,1)S(1)}, u32[]{:S(2)}, u32[]{:S(2)}) %collective-permute-start.3) | collective-permute-done | bytes 458784 | tf_op jit(solution)/shard_map/g3b/ppermute | solution.py:36
  26.7 5.8 %pack.1 = bf16[256,4480]{1,0:T(8,128)(2,1)} custom-call(s32[1]{0:T(128)} %bitcast.where, f32[2,128]{1,0:T(2,128)} %pad_maximum_fusion.meta, bf16[128,3584]{1,0:T(8,128)(2,1)} %refs_0_.1, bf16[128,3584]{1,0:T(8,128)(2,1)} %refs_7_.1), custom_call_target="tpu_custom_call" | custom-call | flops 5637144576 | bytes 33038368 | tf_op jit(solution)/shard_map/pack/pallas_call | solution.py:56
  37.1 7.6 %collective-permute-done.8.refs_9_ = bf16[64,3584]{1,0:T(8,128)(2,1)} collective-permute-done((bf16[64,3584]{1,0:T(8,128)(2,1)S(1)}, bf16[64,3584]{1,0:T(8,128)(2,1)}, u32[]{:S(2)}, u32[]{:S(2)}) %collective-permute-start.8) | collective-permute-done | bytes 458784 | tf_op jit(solution)/shard_map/g1b/ppermute | solution.py:36
  47.7 6.8 %collective-permute-done.5.refs_3_ = bf16[64,3584]{1,0:T(8,128)(2,1)S(1)} collective-permute-done((bf16[64,3584]{1,0:T(8,128)(2,1)S(1)}, bf16[64,3584]{1,0:T(8,128)(2,1)S(1)}, u32[]{:S(2)}, u32[]{:S(2)}) %collective-permute-start.5) | collective-permute-done | bytes 458784 | tf_op jit(solution)/shard_map/xt/ppermute | solution.py:36
  55.9 7.6 %all-to-all-start = ((bf16[16,16,4480]{2,1,0:T(8,128)(2,1)}), bf16[16,16,4480]{2,1,0:T(8,128)(2,1)S(1)}, u32[]{:S(2)}, u32[]{:S(2)}) async-start(bf16[16,16,4480]{2,1,0:T(8,128)(2,1)} %bitcast.24), calls=%async_computation | async-start | bytes 4587520 | tf_op jit(solution)/shard_map/msg/all_to_all | solution.py:697
  63.5 3.9 %collective-permute-start.13 = (bf16[3584,256]{1,0:T(8,128)(2,1)}, bf16[3584,256]{1,0:T(8,128)(2,1)}, u32[]{:S(2)}, u32[]{:S(2)}) collective-permute-start(bf16[3584,256]{1,0:T(8,128)(2,1)} %bitcast.25), channel_id=1, source_target_pairs={{0,1},{1,0},{2,3},{3,2},{4,5},{5,4},{6,7},{7,6},{8,9},{9,8},{10,11... | collective-permute-start | bytes 5505032 | tf_op jit(solution)/shard_map/swap_expert/ppermute | solution.py:45
  67.9 13.7 %shared_weights.1 = (bf16[3584,128]{1,0:T(8,128)(2,1)}, bf16[3584,128]{1,0:T(8,128)(2,1)}, bf16[128,3584]{1,0:T(8,128)(2,1)}, bf16[3584,128]{1,0:T(8,128)(2,1)},...) custom-call(bf16[128,3584]{1,0:T(8,128)(2,1)} %refs_0_.1, ...), custom_call_target="tpu_custom_call" | custom-call | flops 45097156608 | bytes 150994944 | tf_op jit(solution)/shard_map/shared_weights/pallas_call | solution.py:56
  83.6 6.7 %shared_rows.1 = (bf16[128,3584]{1,0:T(8,128)(2,1)}, bf16[128,3584]{1,0:T(8,128)(2,1)}, bf16[128,3584]{1,0:T(8,128)(2,1)}, bf16[128,3584]{1,0:T(8,128)(2,1)}) custom-call(bf16[3584,128]{1,0:T(8,128)(2,1)} %go.1, bf16[3584,128]{1,0:T(8,128)(2,1)} %uo.1, bf16[3584,384]{1,0:T(8,128)(2,1)} %collective-permute-done.12.refs_17_.came, ...), custom_call_target="tpu_custom_call" | custom-call | flops 37580963840 | bytes 175636480 | tf_op jit(solution)/shard_map/shared_rows/pallas_call | solution.py:56
  94.0 4.8 %grad_pack.1 = bf16[3584,384]{1,0:T(8,128)(2,1)} custom-call(bf16[3584,128]{1,0:T(8,128)(2,1)} %get-tuple-element.75.g0, bf16[3584,128]{1,0:T(8,128)(2,1)} %get-tuple-element.76.u0, bf16[128,3584]{1,0:T(8,128)(2,1)} %get-tuple-element.77.d0, bf16[3584,128]{1,0:T(8,128)(2,1)} %copy-done.5, bf16[3584,128]{1,0:T(8,128)(2,1)} %collective-permute-done.17.u1, ...), custom_call_target="tpu_custom_call" | custom-call | flops 68812 | bytes 412876 | tf_op jit(solution)/shard_map/grad_pack/pallas_call | solution.py:56
  100.2 7.6 %all-to-all-start.1 = ((bf16[16,224,384]{2,1,0:T(8,128)(2,1)}), bf16[16,224,384]{2,1,0:T(8,128)(2,1)S(1)}, u32[]{:S(2)}, u32[]{:S(2)}) async-start(bf16[16,224,384]{2,1,0:T(8,128)(2,1)} %bitcast.20), calls=%async_computation.1 | async-start | bytes 5505024 | tf_op jit(solution)/shard_map/scatter/all_to_all | solution.py:697
  107.8 4.2 %regroup.1 = (bf16[80,7168]{1,0:T(8,128)(2,1)}, bf16[80,7168]{1,0:T(8,128)(2,1)}) custom-call(bf16[256,4480]{1,0:T(8,128)(2,1)} %bitcast.22), custom_call_target="tpu_custom_call" | custom-call | flops 36700160 | bytes 229376 | tf_op jit(solution)/shard_map/regroup/pallas_call | solution.py:56
  116.2 25.1 %collective-permute-done.22.refs_2_ = bf16[80,7168]{1,0:T(8,128)(2,1)} collective-permute-done((bf16[80,7168]{1,0:T(8,128)(2,1)}, bf16[80,7168]{1,0:T(8,128)(2,1)}, u32[]{:S(2)}, u32[]{:S(2)}) %collective-permute-start.22) | collective-permute-done | bytes 1146912 | tf_op jit(solution)/shard_map/r2/ppermute | solution.py:705
  142.5 11.0 %routed_rows0.1 = (bf16[80,3584]{1,0:T(8,128)(2,1)}, bf16[80,3584]{1,0:T(8,128)(2,1)}, bf16[80,3584]{1,0:T(8,128)(2,1)}, bf16[240,256]{1,0:T(8,128)(2,1)}, bf16[...) custom-call(bf16[80,7168]{1,0:T(8,128)(2,1)} %get-tuple-element.85.refs_0_, ...), custom_call_target="tpu_custom_call" | custom-call | flops 220200960 | bytes 1017446 | tf_op jit(solution)/shard_map/routed_rows0/pallas_call | solution.py:56
  161.4 7.6 %all-to-all-start.2 = ((bf16[16,224,384]{2,1,0:T(8,128)(2,1)}), bf16[16,224,384]{2,1,0:T(8,128)(2,1)S(1)}, u32[]{:S(2)}, u32[]{:S(2)}) async-start(bf16[16,224,384]{2,1,0:T(8,128)(2,1)} %grad_sum.1), calls=%async_computation.2 | async-start | bytes 5505024 | tf_op jit(solution)/shard_map/gather/all_to_all | solution.py:697
  169.0 9.4 %routed_rows1.1 = (bf16[80,3584]{1,0:T(8,128)(2,1)}, bf16[80,256]{1,0:T(8,128)(2,1)}, bf16[80,256]{1,0:T(8,128)(2,1)}, bf16[80,256]{1,0:T(8,128)(2,1)}, bf16[80,7936]{1,0:T(8,128)(2,1)}) custom-call(bf16[80,7168]{1,0:T(8,128)(2,1)} %collective-permute-done.25.refs_0_, bf16[3584,256]{1,0:T(8,128)(2,1)} %bitcast.27, ...), custom_call_target="tpu_custom_call" | custom-call | flops 29360128000 | bytes 282460160 | tf_op jit(solution)/shard_map/routed_rows1/pallas_call | solution.py:56
  179.2 22.2 %all-to-all-done.2 = bf16[16,224,384]{2,1,0:T(8,128)(2,1)S(1)} async-done(((bf16[16,224,384]{2,1,0:T(8,128)(2,1)}), bf16[16,224,384]{2,1,0:T(8,128)(2,1)S(1)}, u32[]{:S(2)}, u32[]{:S(2)}) %all-to-all-start.2) | async-done | bytes 2752544 | tf_op jit(solution)/shard_map/gather/all_to_all | solution.py:697
  202.3 4.4 %return_pack.1 = bf16[128,4480]{1,0:T(8,128)(2,1)} custom-call(bf16[80,3584]{1,0:T(8,128)(2,1)} %get-tuple-element.91.b0, bf16[80,3584]{1,0:T(8,128)(2,1)} %copy-done.6, bf16[80,3584]{1,0:T(8,128)(2,1)} %collective-permute-done.24.b2, bf16[80,3584]{1,0:T(8,128)(2,1)} %collective-permute-done.26.b3), custom_call_target="tpu_custom_call" | custom-call | flops 14680064 | bytes 172032 | tf_op jit(solution)/shard_map/return_pack/pallas_call | solution.py:56
  206.7 6.7 %collective-permute-start.27 = (bf16[240,7936]{1,0:T(8,128)(2,1)}, bf16[240,7936]{1,0:T(8,128)(2,1)}, u32[]{:S(2)}, u32[]{:S(2)}) collective-permute-start(bf16[240,7936]{1,0:T(8,128)(2,1)} %get-tuple-element.101.refs_0_), channel_id=1, source_target_pairs={{0,1},{1,0},{2,3},{3,2},{4,5},{5,4},{6,7},{7,6},{8,9},{9,8},{10,11... | collective-permute-start | bytes 11427848 | tf_op jit(solution)/shard_map/swap_bundle/ppermute | solution.py:45
  213.4 4.4 %all-to-all-start.3 = ((bf16[16,8,4480]{2,1,0:T(8,128)(2,1)}), bf16[16,8,4480]{2,1,0:T(8,128)(2,1)}, u32[]{:S(2)}, u32[]{:S(2)}) async-start(bf16[16,8,4480]{2,1,0:T(8,128)(2,1)} %bitcast.23), calls=%async_computation.3 | async-start | bytes 2293760 | tf_op jit(solution)/shard_map/returned/all_to_all | solution.py:697
  218.9 3.8 %grad_unpack.1 = (bf16[3584,128]{1,0:T(8,128)(2,1)}, bf16[3584,128]{1,0:T(8,128)(2,1)}, bf16[128,3584]{1,0:T(8,128)(2,1)}) custom-call(bf16[3584,384]{1,0:T(8,128)(2,1)} %bitcast.21), custom_call_target="tpu_custom_call" | custom-call | flops 68812 | bytes 275251 | tf_op jit(solution)/shard_map/grad_unpack/pallas_call | solution.py:56
  222.7 8.9 %routed_weights.1 = (bf16[3584,256]{1,0:T(8,128)(2,1)}, bf16[3584,256]{1,0:T(8,128)(2,1)}, bf16[256,3584]{1,0:T(8,128)(2,1)}) custom-call(bf16[240,7936]{1,0:T(8,128)(2,1)} %get-tuple-element.101.refs_0_, bf16[80,7936]{1,0:T(8,128)(2,1)} %get-tuple-element.102.refs_1_, bf16[240,7936]{1,0:T(8,128)(2,1)} %collective-permute-done.27.refs_2_, ...), custom_call_target="tpu_custom_call" | custom-call | flops 176160768 | bytes 807731 | tf_op jit(solution)/shard_map/routed_weights/pallas_call | solution.py:56
  231.6 4.3 %all-to-all-done.3 = bf16[16,8,4480]{2,1,0:T(8,128)(2,1)} async-done(((bf16[16,8,4480]{2,1,0:T(8,128)(2,1)}), bf16[16,8,4480]{2,1,0:T(8,128)(2,1)}, u32[]{:S(2)}, u32[]{:S(2)}) %all-to-all-start.3) | async-done | bytes 1146912 | tf_op jit(solution)/shard_map/returned/all_to_all | solution.py:697
  235.8 5.2 %collective-permute-done.29.p2 = bf16[128,3584]{1,0:T(8,128)(2,1)S(1)} collective-permute-done((bf16[128,3584]{1,0:T(8,128)(2,1)}, bf16[128,3584]{1,0:T(8,128)(2,1)S(1)}, u32[]{:S(2)}, u32[]{:S(2)}) %collective-permute-start.29) | collective-permute-done | bytes 917536 | tf_op jit(solution)/shard_map/part/ppermute | solution.py:41
  242.0 4.3 %combine.1 = bf16[128,3584]{1,0:T(8,128)(2,1)} custom-call(s32[1]{0:T(128)} %bitcast.where, f32[2,128]{1,0:T(2,128)} %pad_maximum_fusion.meta, bf16[128,4480]{1,0:T(8,128)(2,1)} %bitcast.13.back, bf16[128,3584]{1,0:T(8,128)(2,1)} %get-tuple-element.74.p0, bf16[128,3584]{1,0:T(8,128)(2,1)} %collective-permute-done.19.p1, bf16[128,3584]{1,0:T(8,128)(2,1)} %copy-done.3, ...), custom_call_target="tpu_custom_call" | custom-call | flops 11744051 | bytes 286771 | tf_op jit(solution)/shard_map/combine/pallas_call | solution.py:56
  (92 shorter events, 51.1 us)
Async XLA Ops:
  9.3 58.6 %collective-permute-start.12 = (bf16[3584,384]{1,0:T(8,128)(2,1)}, bf16[3584,384]{1,0:T(8,128)(2,1)}, u32[]{:S(2)}, u32[]{:S(2)}) collective-permute-start(bf16[3584,384]{1,0:T(8,128)(2,1)} %stack.1), channel_id=1, source_target_pairs={{0,1},{1,0},{2,3},{3,2},{4,5},{5,4},{6,7},{7,6},{8,9},{9,8},{10,11... | collective-permute-start | bytes 8257544 | tf_op jit(solution)/shard_map/swap_shared/ppermute | solution.py:45
  11.3 15.4 %collective-permute-start.2 = (bf16[64,3584]{1,0:T(8,128)(2,1)}, bf16[64,3584]{1,0:T(8,128)(2,1)S(1)}, u32[]{:S(2)}, u32[]{:S(2)}) collective-permute-start(bf16[64,3584]{1,0:T(8,128)(2,1)} %get-tuple-element.118), channel_id=1, source_target_pairs={{0,6},{2,0},{4,2},{6,4},{1,7},{3,1},{5,3},{7,5},{8,14},{10,8},{12,... | collective-permute-start | bytes 1376264 | tf_op jit(solution)/shard_map/g1t/ppermute | solution.py:36
  15.7 19.1 %collective-permute-start.4 = (bf16[64,3584]{1,0:T(8,128)(2,1)S(1)}, bf16[64,3584]{1,0:T(8,128)(2,1)S(1)}, u32[]{:S(2)}, u32[]{:S(2)}) collective-permute-start(bf16[64,3584]{1,0:T(8,128)(2,1)S(1)} %get-tuple-element.119), channel_id=1, source_target_pairs={{0,6},{2,0},{4,2},{6,4},{1,7},{3,1},{5,3},{7,5},{8,14},{10,8},{12,... | collective-permute-start | bytes 1376264 | tf_op jit(solution)/shard_map/x1b/ppermute | solution.py:36
  17.0 19.1 %collective-permute-start.7 = (bf16[64,3584]{1,0:T(8,128)(2,1)S(1)}, bf16[64,3584]{1,0:T(8,128)(2,1)S(1)}, u32[]{:S(2)}, u32[]{:S(2)}) collective-permute-start(bf16[64,3584]{1,0:T(8,128)(2,1)S(1)} %get-tuple-element.120), channel_id=1, source_target_pairs={{0,2},{2,4},{4,6},{6,0},{1,3},{3,5},{5,7},{7,1},{8,10},{10,12},{12... | collective-permute-start | bytes 1376264 | tf_op jit(solution)/shard_map/x3t/ppermute | solution.py:36
  25.4 19.3 %collective-permute-start.8 = (bf16[64,3584]{1,0:T(8,128)(2,1)S(1)}, bf16[64,3584]{1,0:T(8,128)(2,1)}, u32[]{:S(2)}, u32[]{:S(2)}) collective-permute-start(bf16[64,3584]{1,0:T(8,128)(2,1)S(1)} %get-tuple-element.117), channel_id=1, source_target_pairs={{0,6},{2,0},{4,2},{6,4},{1,7},{3,1},{5,3},{7,5},{8,14},{10,8},{12,... | collective-permute-start | bytes 1376264 | tf_op jit(solution)/shard_map/g1b/ppermute | solution.py:36
  32.6 22.0 %collective-permute-start.5 = (bf16[64,3584]{1,0:T(8,128)(2,1)S(1)}, bf16[64,3584]{1,0:T(8,128)(2,1)S(1)}, u32[]{:S(2)}, u32[]{:S(2)}) collective-permute-start(bf16[64,3584]{1,0:T(8,128)(2,1)S(1)} %collective-permute-done.refs_1_), channel_id=1, source_target_pairs={{0,6},{2,0},{4,2},{6,4},{1,7},{3,1},{5,3},{7,5},{8,14},{10,8},{12,... | collective-permute-start | bytes 1376264 | tf_op jit(solution)/shard_map/xt/ppermute | solution.py:36
  34.8 28.7 %collective-permute-start.11 = (bf16[64,3584]{1,0:T(8,128)(2,1)}, bf16[64,3584]{1,0:T(8,128)(2,1)}, u32[]{:S(2)}, u32[]{:S(2)}) collective-permute-start(bf16[64,3584]{1,0:T(8,128)(2,1)} %get-tuple-element.118), channel_id=1, source_target_pairs={{0,2},{2,4},{4,6},{6,0},{1,3},{3,5},{5,7},{7,1},{8,10},{10,12},{12... | collective-permute-start | bytes 1376264 | tf_op jit(solution)/shard_map/g3t/ppermute | solution.py:36
  36.1 31.3 %collective-permute-start.6 = (bf16[64,3584]{1,0:T(8,128)(2,1)}, bf16[64,3584]{1,0:T(8,128)(2,1)}, u32[]{:S(2)}, u32[]{:S(2)}) collective-permute-start(bf16[64,3584]{1,0:T(8,128)(2,1)} %collective-permute-done.1.refs_6_), channel_id=1, source_target_pairs={{0,2},{2,4},{4,6},{6,0},{1,3},{3,5},{5,7},{7,1},{8,10},{10,12},{12... | collective-permute-start | bytes 1376264 | tf_op jit(solution)/shard_map/xb/ppermute | solution.py:36
  44.7 22.7 %collective-permute-start.9 = (bf16[64,3584]{1,0:T(8,128)(2,1)S(1)}, bf16[64,3584]{1,0:T(8,128)(2,1)}, u32[]{:S(2)}, u32[]{:S(2)}) collective-permute-start(bf16[64,3584]{1,0:T(8,128)(2,1)S(1)} %collective-permute-done.2.refs_8_), channel_id=1, source_target_pairs={{0,6},{2,0},{4,2},{6,4},{1,7},{3,1},{5,3},{7,5},{8,14},{10,8},{12,... | collective-permute-start | bytes 1376264 | tf_op jit(solution)/shard_map/gt/ppermute | solution.py:36
  55.9 43.0 %all-to-all-start = ((bf16[16,16,4480]{2,1,0:T(8,128)(2,1)}), bf16[16,16,4480]{2,1,0:T(8,128)(2,1)S(1)}, u32[]{:S(2)}, u32[]{:S(2)}) async-start(bf16[16,16,4480]{2,1,0:T(8,128)(2,1)} %bitcast.24), calls=%async_computation | async-start | bytes 4587520 | tf_op jit(solution)/shard_map/msg/all_to_all | solution.py:697
  63.5 18.1 %collective-permute-start.13 = (bf16[3584,256]{1,0:T(8,128)(2,1)}, bf16[3584,256]{1,0:T(8,128)(2,1)}, u32[]{:S(2)}, u32[]{:S(2)}) collective-permute-start(bf16[3584,256]{1,0:T(8,128)(2,1)} %bitcast.25), channel_id=1, source_target_pairs={{0,1},{1,0},{2,3},{3,2},{4,5},{5,4},{6,7},{7,6},{8,9},{9,8},{10,11... | collective-permute-start | bytes 5505032 | tf_op jit(solution)/shard_map/swap_expert/ppermute | solution.py:45
  90.3 23.5 %collective-permute-start.19 = (bf16[128,3584]{1,0:T(8,128)(2,1)}, bf16[128,3584]{1,0:T(8,128)(2,1)}, u32[]{:S(2)}, u32[]{:S(2)}) collective-permute-start(bf16[128,3584]{1,0:T(8,128)(2,1)} %get-tuple-element.83), channel_id=1, source_target_pairs={{0,2},{2,4},{4,6},{6,0},{1,3},{3,5},{5,7},{7,1},{8,10},{10,12},{12... | collective-permute-start | bytes 2752520 | tf_op jit(solution)/shard_map/part/ppermute | solution.py:41
  90.4 23.4 %collective-permute-start.20 = (bf16[128,3584]{1,0:T(8,128)(2,1)}, bf16[128,3584]{1,0:T(8,128)(2,1)}, u32[]{:S(2)}, u32[]{:S(2)}) collective-permute-start(bf16[128,3584]{1,0:T(8,128)(2,1)} %get-tuple-element.84), channel_id=1, source_target_pairs={{0,6},{2,0},{4,2},{6,4},{1,7},{3,1},{5,3},{7,5},{8,14},{10,8},{12,... | collective-permute-start | bytes 2752520 | tf_op jit(solution)/shard_map/part/ppermute | solution.py:41
  100.2 55.9 %all-to-all-start.1 = ((bf16[16,224,384]{2,1,0:T(8,128)(2,1)}), bf16[16,224,384]{2,1,0:T(8,128)(2,1)S(1)}, u32[]{:S(2)}, u32[]{:S(2)}) async-start(bf16[16,224,384]{2,1,0:T(8,128)(2,1)} %bitcast.20), calls=%async_computation.1 | async-start | bytes 5505024 | tf_op jit(solution)/shard_map/scatter/all_to_all | solution.py:697
  113.8 27.4 %collective-permute-start.22 = (bf16[80,7168]{1,0:T(8,128)(2,1)}, bf16[80,7168]{1,0:T(8,128)(2,1)}, u32[]{:S(2)}, u32[]{:S(2)}) collective-permute-start(bf16[80,7168]{1,0:T(8,128)(2,1)} %get-tuple-element.94), channel_id=1, source_target_pairs={{0,6},{2,4},{4,2},{6,0},{1,7},{3,5},{5,3},{7,1},{8,14},{10,12},{12... | collective-permute-start | bytes 3440648 | tf_op jit(solution)/shard_map/r2/ppermute | solution.py:705
  116.2 25.6 %collective-permute-start.21 = (bf16[80,7168]{1,0:T(8,128)(2,1)}, bf16[80,7168]{1,0:T(8,128)(2,1)}, u32[]{:S(2)}, u32[]{:S(2)}) collective-permute-start(bf16[80,7168]{1,0:T(8,128)(2,1)} %get-tuple-element.85.refs_0_), channel_id=1, source_target_pairs={{0,2},{2,0},{4,6},{6,4},{1,3},{3,1},{5,7},{7,5},{8,10},{10,8},{12,... | collective-permute-start | bytes 3440648 | tf_op jit(solution)/shard_map/r1/ppermute | solution.py:705
  141.8 27.2 %collective-permute-start.25 = (bf16[80,7168]{1,0:T(8,128)(2,1)}, bf16[80,7168]{1,0:T(8,128)(2,1)}, u32[]{:S(2)}, u32[]{:S(2)}) collective-permute-start(bf16[80,7168]{1,0:T(8,128)(2,1)} %get-tuple-element.94), channel_id=1, source_target_pairs={{0,4},{2,6},{4,0},{6,2},{1,5},{3,7},{5,1},{7,3},{8,12},{10,14},{12... | collective-permute-start | bytes 3440648 | tf_op jit(solution)/shard_map/r3/ppermute | solution.py:705
  153.4 48.0 %collective-permute-start.23 = (bf16[80,3584]{1,0:T(8,128)(2,1)}, bf16[80,3584]{1,0:T(8,128)(2,1)S(1)}, u32[]{:S(2)}, u32[]{:S(2)}) collective-permute-start(bf16[80,3584]{1,0:T(8,128)(2,1)} %get-tuple-element.92), channel_id=1, source_target_pairs={{0,2},{2,0},{4,6},{6,4},{1,3},{3,1},{5,7},{7,5},{8,10},{10,8},{12,... | collective-permute-start | bytes 1720328 | tf_op jit(solution)/shard_map/b1/ppermute | solution.py:705
  154.9 46.5 %collective-permute-start.24 = (bf16[80,3584]{1,0:T(8,128)(2,1)}, bf16[80,3584]{1,0:T(8,128)(2,1)}, u32[]{:S(2)}, u32[]{:S(2)}) collective-permute-start(bf16[80,3584]{1,0:T(8,128)(2,1)} %get-tuple-element.93), channel_id=1, source_target_pairs={{0,6},{2,4},{4,2},{6,0},{1,7},{3,5},{5,3},{7,1},{8,14},{10,12},{12... | collective-permute-start | bytes 1720328 | tf_op jit(solution)/shard_map/b2/ppermute | solution.py:705
  161.4 40.0 %all-to-all-start.2 = ((bf16[16,224,384]{2,1,0:T(8,128)(2,1)}), bf16[16,224,384]{2,1,0:T(8,128)(2,1)S(1)}, u32[]{:S(2)}, u32[]{:S(2)}) async-start(bf16[16,224,384]{2,1,0:T(8,128)(2,1)} %grad_sum.1), calls=%async_computation.2 | async-start | bytes 5505024 | tf_op jit(solution)/shard_map/gather/all_to_all | solution.py:697
  178.5 23.0 %collective-permute-start.26 = (bf16[80,3584]{1,0:T(8,128)(2,1)}, bf16[80,3584]{1,0:T(8,128)(2,1)}, u32[]{:S(2)}, u32[]{:S(2)}) collective-permute-start(bf16[80,3584]{1,0:T(8,128)(2,1)} %get-tuple-element.96), channel_id=1, source_target_pairs={{0,4},{2,6},{4,0},{6,2},{1,5},{3,7},{5,1},{7,3},{8,12},{10,14},{12... | collective-permute-start | bytes 1720328 | tf_op jit(solution)/shard_map/b3/ppermute | solution.py:705
  206.7 15.9 %collective-permute-start.27 = (bf16[240,7936]{1,0:T(8,128)(2,1)}, bf16[240,7936]{1,0:T(8,128)(2,1)}, u32[]{:S(2)}, u32[]{:S(2)}) collective-permute-start(bf16[240,7936]{1,0:T(8,128)(2,1)} %get-tuple-element.101.refs_0_), channel_id=1, source_target_pairs={{0,1},{1,0},{2,3},{3,2},{4,5},{5,4},{6,7},{7,6},{8,9},{9,8},{10,11... | collective-permute-start | bytes 11427848 | tf_op jit(solution)/shard_map/swap_bundle/ppermute | solution.py:45
  213.4 22.4 %all-to-all-start.3 = ((bf16[16,8,4480]{2,1,0:T(8,128)(2,1)}), bf16[16,8,4480]{2,1,0:T(8,128)(2,1)}, u32[]{:S(2)}, u32[]{:S(2)}) async-start(bf16[16,8,4480]{2,1,0:T(8,128)(2,1)} %bitcast.23), calls=%async_computation.3 | async-start | bytes 2293760 | tf_op jit(solution)/shard_map/returned/all_to_all | solution.py:697
  217.8 23.2 %collective-permute-start.29 = (bf16[128,3584]{1,0:T(8,128)(2,1)}, bf16[128,3584]{1,0:T(8,128)(2,1)S(1)}, u32[]{:S(2)}, u32[]{:S(2)}) collective-permute-start(bf16[128,3584]{1,0:T(8,128)(2,1)} %get-tuple-element.112), channel_id=1, source_target_pairs={{0,4},{2,6},{4,0},{6,2},{1,5},{3,7},{5,1},{7,3},{8,12},{10,14},{12... | collective-permute-start | bytes 2752520 | tf_op jit(solution)/shard_map/part/ppermute | solution.py:41
  (25 other events, 261.2 us)

commit v2 on v1

--- a/solution.py
+++ b/solution.py
@@ -9,7 +9,7 @@
 
 CAP = 5
 RET = 8
-TILE = 512
+TILE = 896
 WEIGHT = {'pack': 8, 'shared_weights': 8, 'routed_rows0': .05, 'routed_rows1': 20, 'routed_weights': .05, 'shared_rows': 20, 'regroup': .05, 'grad_pack': .05, 'return_pack': .05, 'combine': .05, 'grad_unpack': .05}
 F32 = jnp.float32
 BF16 = jnp.bfloat16

time: 247 us -> 246 us (level)
  transfers between devices with their start and end apart: 34 -> 34, of which waited for: 11 -> 11; matrix products, arithmetic and copies ran while one was open for 1% -> 1% of each run, Pallas kernels for 31% -> 30%
where the time goes in v2:
time: 246 us; the launch traced here: 245 us
  waiting for transfers between devices  85.1 us (35%)
  Pallas kernels  82.2 us (33%)
  starting transfers between devices  68.6 us (28%)
  local copies, waits for them, and re-layouts  7.72 us (3%)
    pallas_call x13, Pallas kernels, call(): pl.pallas_call(body, out_shape=out_shape, in_specs=specs, out_specs=out_s...  82.2 us
    all_to_all x4, waiting for transfers between devices, exchange(): return lax.all_to_all(v, axes, split_axis=0, concat_axis=0, tiled=True)  27.2 us
    all_to_all x4, starting transfers between devices, exchange(): return lax.all_to_all(v, axes, split_axis=0, concat_axis=0, tiled=True)  27.1 us
    ppermute x6, waiting for transfers between devices, pairs_y(): lax.ppermute(v, 'y', list(enumerate(order)))  25.6 us
    ppermute x12, waiting for transfers between devices, from_y(): return lax.ppermute(v, 'y', [(i, (i - k) % n) for i in range(n)])  25.3 us
    ppermute x12, starting transfers between devices, from_y(): return lax.ppermute(v, 'y', [(i, (i - k) % n) for i in range(n)])  17.1 us
    ppermute x9, starting transfers between devices, swap_core(): return lax.ppermute(v, 'c', [(0, 1), (1, 0)])  14 us
    ppermute x3, waiting for transfers between devices, to_y(): return lax.ppermute(v, 'y', [(i, (i + k) % n) for i in range(n)])  6.99 us
  transfers between devices with their start and end apart: 34, of which 11 were waited for; matrix products, arithmetic and copies ran while one was open for 1% of the time, Pallas kernels for 30%

profile of v2, /device:TPU:1, one launch (start us, length us, event | category | flops | bytes accessed | tf_op | source)
XLA Modules:
  0.0 245.0 jit_solution(12743252791384608334)
XLA Ops:
  17.2 8.3 %collective-permute-done.3.refs_13_ = bf16[64,3584]{1,0:T(8,128)(2,1)S(1)} collective-permute-done((bf16[64,3584]{1,0:T(8,128)(2,1)S(1)}, bf16[64,3584]{1,0:T(8,128)(2,1)S(1)}, u32[]{:S(2)}, u32[]{:S(2)}) %collective-permute-start.3) | collective-permute-done | bytes 458784 | tf_op jit(solution)/shard_map/g3b/ppermute | solution.py:36
  26.7 5.4 %pack.1 = bf16[256,4480]{1,0:T(8,128)(2,1)} custom-call(s32[1]{0:T(128)} %bitcast.where, f32[2,128]{1,0:T(2,128)} %pad_maximum_fusion.meta, bf16[128,3584]{1,0:T(8,128)(2,1)} %refs_0_.1, bf16[128,3584]{1,0:T(8,128)(2,1)} %refs_7_.1), custom_call_target="tpu_custom_call" | custom-call | flops 5637144576 | bytes 33038368 | tf_op jit(solution)/shard_map/pack/pallas_call | solution.py:56
  37.1 7.6 %collective-permute-done.8.refs_9_ = bf16[64,3584]{1,0:T(8,128)(2,1)} collective-permute-done((bf16[64,3584]{1,0:T(8,128)(2,1)S(1)}, bf16[64,3584]{1,0:T(8,128)(2,1)}, u32[]{:S(2)}, u32[]{:S(2)}) %collective-permute-start.8) | collective-permute-done | bytes 458784 | tf_op jit(solution)/shard_map/g1b/ppermute | solution.py:36
  47.7 6.8 %collective-permute-done.5.refs_3_ = bf16[64,3584]{1,0:T(8,128)(2,1)S(1)} collective-permute-done((bf16[64,3584]{1,0:T(8,128)(2,1)S(1)}, bf16[64,3584]{1,0:T(8,128)(2,1)S(1)}, u32[]{:S(2)}, u32[]{:S(2)}) %collective-permute-start.5) | collective-permute-done | bytes 458784 | tf_op jit(solution)/shard_map/xt/ppermute | solution.py:36
  55.9 7.6 %all-to-all-start = ((bf16[16,16,4480]{2,1,0:T(8,128)(2,1)}), bf16[16,16,4480]{2,1,0:T(8,128)(2,1)S(1)}, u32[]{:S(2)}, u32[]{:S(2)}) async-start(bf16[16,16,4480]{2,1,0:T(8,128)(2,1)} %bitcast.24), calls=%async_computation | async-start | bytes 4587520 | tf_op jit(solution)/shard_map/msg/all_to_all | solution.py:697
  63.5 3.9 %collective-permute-start.13 = (bf16[3584,256]{1,0:T(8,128)(2,1)}, bf16[3584,256]{1,0:T(8,128)(2,1)}, u32[]{:S(2)}, u32[]{:S(2)}) collective-permute-start(bf16[3584,256]{1,0:T(8,128)(2,1)} %bitcast.25), channel_id=1, source_target_pairs={{0,1},{1,0},{2,3},{3,2},{4,5},{5,4},{6,7},{7,6},{8,9},{9,8},{10,11... | collective-permute-start | bytes 5505032 | tf_op jit(solution)/shard_map/swap_expert/ppermute | solution.py:45
  67.9 13.0 %shared_weights.1 = (bf16[3584,128]{1,0:T(8,128)(2,1)}, bf16[3584,128]{1,0:T(8,128)(2,1)}, bf16[128,3584]{1,0:T(8,128)(2,1)}, bf16[3584,128]{1,0:T(8,128)(2,1)},...) custom-call(bf16[128,3584]{1,0:T(8,128)(2,1)} %refs_0_.1, ...), custom_call_target="tpu_custom_call" | custom-call | flops 45097156608 | bytes 150994944 | tf_op jit(solution)/shard_map/shared_weights/pallas_call | solution.py:56
  82.9 6.5 %shared_rows.1 = (bf16[128,3584]{1,0:T(8,128)(2,1)}, bf16[128,3584]{1,0:T(8,128)(2,1)}, bf16[128,3584]{1,0:T(8,128)(2,1)}, bf16[128,3584]{1,0:T(8,128)(2,1)}) custom-call(bf16[3584,128]{1,0:T(8,128)(2,1)} %go.1, bf16[3584,128]{1,0:T(8,128)(2,1)} %uo.1, bf16[3584,384]{1,0:T(8,128)(2,1)} %collective-permute-done.12.refs_17_.came, ...), custom_call_target="tpu_custom_call" | custom-call | flops 37580963840 | bytes 175636480 | tf_op jit(solution)/shard_map/shared_rows/pallas_call | solution.py:56
  93.1 4.8 %grad_pack.1 = bf16[3584,384]{1,0:T(8,128)(2,1)} custom-call(bf16[3584,128]{1,0:T(8,128)(2,1)} %get-tuple-element.75.g0, bf16[3584,128]{1,0:T(8,128)(2,1)} %get-tuple-element.76.u0, bf16[128,3584]{1,0:T(8,128)(2,1)} %get-tuple-element.77.d0, bf16[3584,128]{1,0:T(8,128)(2,1)} %copy-done.5, bf16[3584,128]{1,0:T(8,128)(2,1)} %collective-permute-done.17.u1, ...), custom_call_target="tpu_custom_call" | custom-call | flops 68812 | bytes 412876 | tf_op jit(solution)/shard_map/grad_pack/pallas_call | solution.py:56
  99.3 7.6 %all-to-all-start.1 = ((bf16[16,224,384]{2,1,0:T(8,128)(2,1)}), bf16[16,224,384]{2,1,0:T(8,128)(2,1)S(1)}, u32[]{:S(2)}, u32[]{:S(2)}) async-start(bf16[16,224,384]{2,1,0:T(8,128)(2,1)} %bitcast.20), calls=%async_computation.1 | async-start | bytes 5505024 | tf_op jit(solution)/shard_map/scatter/all_to_all | solution.py:697
  106.9 4.2 %regroup.1 = (bf16[80,7168]{1,0:T(8,128)(2,1)}, bf16[80,7168]{1,0:T(8,128)(2,1)}) custom-call(bf16[256,4480]{1,0:T(8,128)(2,1)} %bitcast.22), custom_call_target="tpu_custom_call" | custom-call | flops 36700160 | bytes 229376 | tf_op jit(solution)/shard_map/regroup/pallas_call | solution.py:56
  115.3 25.1 %collective-permute-done.22.refs_2_ = bf16[80,7168]{1,0:T(8,128)(2,1)} collective-permute-done((bf16[80,7168]{1,0:T(8,128)(2,1)}, bf16[80,7168]{1,0:T(8,128)(2,1)}, u32[]{:S(2)}, u32[]{:S(2)}) %collective-permute-start.22) | collective-permute-done | bytes 1146912 | tf_op jit(solution)/shard_map/r2/ppermute | solution.py:705
  141.5 10.7 %routed_rows0.1 = (bf16[80,3584]{1,0:T(8,128)(2,1)}, bf16[80,3584]{1,0:T(8,128)(2,1)}, bf16[80,3584]{1,0:T(8,128)(2,1)}, bf16[240,256]{1,0:T(8,128)(2,1)}, bf16[...) custom-call(bf16[80,7168]{1,0:T(8,128)(2,1)} %get-tuple-element.85.refs_0_, ...), custom_call_target="tpu_custom_call" | custom-call | flops 220200960 | bytes 1017446 | tf_op jit(solution)/shard_map/routed_rows0/pallas_call | solution.py:56
  160.2 7.6 %all-to-all-start.2 = ((bf16[16,224,384]{2,1,0:T(8,128)(2,1)}), bf16[16,224,384]{2,1,0:T(8,128)(2,1)S(1)}, u32[]{:S(2)}, u32[]{:S(2)}) async-start(bf16[16,224,384]{2,1,0:T(8,128)(2,1)} %grad_sum.1), calls=%async_computation.2 | async-start | bytes 5505024 | tf_op jit(solution)/shard_map/gather/all_to_all | solution.py:697
  167.8 9.1 %routed_rows1.1 = (bf16[80,3584]{1,0:T(8,128)(2,1)}, bf16[80,256]{1,0:T(8,128)(2,1)}, bf16[80,256]{1,0:T(8,128)(2,1)}, bf16[80,256]{1,0:T(8,128)(2,1)}, bf16[80,7936]{1,0:T(8,128)(2,1)}) custom-call(bf16[80,7168]{1,0:T(8,128)(2,1)} %collective-permute-done.25.refs_0_, bf16[3584,256]{1,0:T(8,128)(2,1)} %bitcast.27, ...), custom_call_target="tpu_custom_call" | custom-call | flops 29360128000 | bytes 282460160 | tf_op jit(solution)/shard_map/routed_rows1/pallas_call | solution.py:56
  177.6 22.6 %all-to-all-done.2 = bf16[16,224,384]{2,1,0:T(8,128)(2,1)S(1)} async-done(((bf16[16,224,384]{2,1,0:T(8,128)(2,1)}), bf16[16,224,384]{2,1,0:T(8,128)(2,1)S(1)}, u32[]{:S(2)}, u32[]{:S(2)}) %all-to-all-start.2) | async-done | bytes 2752544 | tf_op jit(solution)/shard_map/gather/all_to_all | solution.py:697
  201.1 4.4 %return_pack.1 = bf16[128,4480]{1,0:T(8,128)(2,1)} custom-call(bf16[80,3584]{1,0:T(8,128)(2,1)} %get-tuple-element.91.b0, bf16[80,3584]{1,0:T(8,128)(2,1)} %copy-done.6, bf16[80,3584]{1,0:T(8,128)(2,1)} %collective-permute-done.24.b2, bf16[80,3584]{1,0:T(8,128)(2,1)} %collective-permute-done.26.b3), custom_call_target="tpu_custom_call" | custom-call | flops 14680064 | bytes 172032 | tf_op jit(solution)/shard_map/return_pack/pallas_call | solution.py:56
  205.5 6.7 %collective-permute-start.27 = (bf16[240,7936]{1,0:T(8,128)(2,1)}, bf16[240,7936]{1,0:T(8,128)(2,1)}, u32[]{:S(2)}, u32[]{:S(2)}) collective-permute-start(bf16[240,7936]{1,0:T(8,128)(2,1)} %get-tuple-element.101.refs_0_), channel_id=1, source_target_pairs={{0,1},{1,0},{2,3},{3,2},{4,5},{5,4},{6,7},{7,6},{8,9},{9,8},{10,11... | collective-permute-start | bytes 11427848 | tf_op jit(solution)/shard_map/swap_bundle/ppermute | solution.py:45
  212.2 4.4 %all-to-all-start.3 = ((bf16[16,8,4480]{2,1,0:T(8,128)(2,1)}), bf16[16,8,4480]{2,1,0:T(8,128)(2,1)}, u32[]{:S(2)}, u32[]{:S(2)}) async-start(bf16[16,8,4480]{2,1,0:T(8,128)(2,1)} %bitcast.23), calls=%async_computation.3 | async-start | bytes 2293760 | tf_op jit(solution)/shard_map/returned/all_to_all | solution.py:697
  217.7 3.8 %grad_unpack.1 = (bf16[3584,128]{1,0:T(8,128)(2,1)}, bf16[3584,128]{1,0:T(8,128)(2,1)}, bf16[128,3584]{1,0:T(8,128)(2,1)}) custom-call(bf16[3584,384]{1,0:T(8,128)(2,1)} %bitcast.21), custom_call_target="tpu_custom_call" | custom-call | flops 68812 | bytes 275251 | tf_op jit(solution)/shard_map/grad_unpack/pallas_call | solution.py:56
  221.4 8.5 %routed_weights.1 = (bf16[3584,256]{1,0:T(8,128)(2,1)}, bf16[3584,256]{1,0:T(8,128)(2,1)}, bf16[256,3584]{1,0:T(8,128)(2,1)}) custom-call(bf16[240,7936]{1,0:T(8,128)(2,1)} %get-tuple-element.101.refs_0_, bf16[80,7936]{1,0:T(8,128)(2,1)} %get-tuple-element.102.refs_1_, bf16[240,7936]{1,0:T(8,128)(2,1)} %collective-permute-done.27.refs_2_, ...), custom_call_target="tpu_custom_call" | custom-call | flops 176160768 | bytes 807731 | tf_op jit(solution)/shard_map/routed_weights/pallas_call | solution.py:56
  230.0 4.6 %all-to-all-done.3 = bf16[16,8,4480]{2,1,0:T(8,128)(2,1)} async-done(((bf16[16,8,4480]{2,1,0:T(8,128)(2,1)}), bf16[16,8,4480]{2,1,0:T(8,128)(2,1)}, u32[]{:S(2)}, u32[]{:S(2)}) %all-to-all-start.3) | async-done | bytes 1146912 | tf_op jit(solution)/shard_map/returned/all_to_all | solution.py:697
  234.6 5.2 %collective-permute-done.29.p2 = bf16[128,3584]{1,0:T(8,128)(2,1)S(1)} collective-permute-done((bf16[128,3584]{1,0:T(8,128)(2,1)}, bf16[128,3584]{1,0:T(8,128)(2,1)S(1)}, u32[]{:S(2)}, u32[]{:S(2)}) %collective-permute-start.29) | collective-permute-done | bytes 917536 | tf_op jit(solution)/shard_map/part/ppermute | solution.py:41
  240.7 4.3 %combine.1 = bf16[128,3584]{1,0:T(8,128)(2,1)} custom-call(s32[1]{0:T(128)} %bitcast.where, f32[2,128]{1,0:T(2,128)} %pad_maximum_fusion.meta, bf16[128,4480]{1,0:T(8,128)(2,1)} %bitcast.13.back, bf16[128,3584]{1,0:T(8,128)(2,1)} %get-tuple-element.74.p0, bf16[128,3584]{1,0:T(8,128)(2,1)} %collective-permute-done.19.p1, bf16[128,3584]{1,0:T(8,128)(2,1)} %copy-done.3, ...), custom_call_target="tpu_custom_call" | custom-call | flops 11744051 | bytes 286771 | tf_op jit(solution)/shard_map/combine/pallas_call | solution.py:56
  (92 shorter events, 51.5 us)
Async XLA Ops:
  9.3 58.6 %collective-permute-start.12 = (bf16[3584,384]{1,0:T(8,128)(2,1)}, bf16[3584,384]{1,0:T(8,128)(2,1)}, u32[]{:S(2)}, u32[]{:S(2)}) collective-permute-start(bf16[3584,384]{1,0:T(8,128)(2,1)} %stack.1), channel_id=1, source_target_pairs={{0,1},{1,0},{2,3},{3,2},{4,5},{5,4},{6,7},{7,6},{8,9},{9,8},{10,11... | collective-permute-start | bytes 8257544 | tf_op jit(solution)/shard_map/swap_shared/ppermute | solution.py:45
  11.3 15.4 %collective-permute-start.2 = (bf16[64,3584]{1,0:T(8,128)(2,1)}, bf16[64,3584]{1,0:T(8,128)(2,1)S(1)}, u32[]{:S(2)}, u32[]{:S(2)}) collective-permute-start(bf16[64,3584]{1,0:T(8,128)(2,1)} %get-tuple-element.118), channel_id=1, source_target_pairs={{0,6},{2,0},{4,2},{6,4},{1,7},{3,1},{5,3},{7,5},{8,14},{10,8},{12,... | collective-permute-start | bytes 1376264 | tf_op jit(solution)/shard_map/g1t/ppermute | solution.py:36
  15.7 19.1 %collective-permute-start.4 = (bf16[64,3584]{1,0:T(8,128)(2,1)S(1)}, bf16[64,3584]{1,0:T(8,128)(2,1)S(1)}, u32[]{:S(2)}, u32[]{:S(2)}) collective-permute-start(bf16[64,3584]{1,0:T(8,128)(2,1)S(1)} %get-tuple-element.119), channel_id=1, source_target_pairs={{0,6},{2,0},{4,2},{6,4},{1,7},{3,1},{5,3},{7,5},{8,14},{10,8},{12,... | collective-permute-start | bytes 1376264 | tf_op jit(solution)/shard_map/x1b/ppermute | solution.py:36
  17.0 19.1 %collective-permute-start.7 = (bf16[64,3584]{1,0:T(8,128)(2,1)S(1)}, bf16[64,3584]{1,0:T(8,128)(2,1)S(1)}, u32[]{:S(2)}, u32[]{:S(2)}) collective-permute-start(bf16[64,3584]{1,0:T(8,128)(2,1)S(1)} %get-tuple-element.120), channel_id=1, source_target_pairs={{0,2},{2,4},{4,6},{6,0},{1,3},{3,5},{5,7},{7,1},{8,10},{10,12},{12... | collective-permute-start | bytes 1376264 | tf_op jit(solution)/shard_map/x3t/ppermute | solution.py:36
  25.4 19.3 %collective-permute-start.8 = (bf16[64,3584]{1,0:T(8,128)(2,1)S(1)}, bf16[64,3584]{1,0:T(8,128)(2,1)}, u32[]{:S(2)}, u32[]{:S(2)}) collective-permute-start(bf16[64,3584]{1,0:T(8,128)(2,1)S(1)} %get-tuple-element.117), channel_id=1, source_target_pairs={{0,6},{2,0},{4,2},{6,4},{1,7},{3,1},{5,3},{7,5},{8,14},{10,8},{12,... | collective-permute-start | bytes 1376264 | tf_op jit(solution)/shard_map/g1b/ppermute | solution.py:36
  32.2 22.4 %collective-permute-start.5 = (bf16[64,3584]{1,0:T(8,128)(2,1)S(1)}, bf16[64,3584]{1,0:T(8,128)(2,1)S(1)}, u32[]{:S(2)}, u32[]{:S(2)}) collective-permute-start(bf16[64,3584]{1,0:T(8,128)(2,1)S(1)} %collective-permute-done.refs_1_), channel_id=1, source_target_pairs={{0,6},{2,0},{4,2},{6,4},{1,7},{3,1},{5,3},{7,5},{8,14},{10,8},{12,... | collective-permute-start | bytes 1376264 | tf_op jit(solution)/shard_map/xt/ppermute | solution.py:36
  34.8 28.7 %collective-permute-start.11 = (bf16[64,3584]{1,0:T(8,128)(2,1)}, bf16[64,3584]{1,0:T(8,128)(2,1)}, u32[]{:S(2)}, u32[]{:S(2)}) collective-permute-start(bf16[64,3584]{1,0:T(8,128)(2,1)} %get-tuple-element.118), channel_id=1, source_target_pairs={{0,2},{2,4},{4,6},{6,0},{1,3},{3,5},{5,7},{7,1},{8,10},{10,12},{12... | collective-permute-start | bytes 1376264 | tf_op jit(solution)/shard_map/g3t/ppermute | solution.py:36
  36.1 31.3 %collective-permute-start.6 = (bf16[64,3584]{1,0:T(8,128)(2,1)}, bf16[64,3584]{1,0:T(8,128)(2,1)}, u32[]{:S(2)}, u32[]{:S(2)}) collective-permute-start(bf16[64,3584]{1,0:T(8,128)(2,1)} %collective-permute-done.1.refs_6_), channel_id=1, source_target_pairs={{0,2},{2,4},{4,6},{6,0},{1,3},{3,5},{5,7},{7,1},{8,10},{10,12},{12... | collective-permute-start | bytes 1376264 | tf_op jit(solution)/shard_map/xb/ppermute | solution.py:36
  44.7 22.7 %collective-permute-start.9 = (bf16[64,3584]{1,0:T(8,128)(2,1)S(1)}, bf16[64,3584]{1,0:T(8,128)(2,1)}, u32[]{:S(2)}, u32[]{:S(2)}) collective-permute-start(bf16[64,3584]{1,0:T(8,128)(2,1)S(1)} %collective-permute-done.2.refs_8_), channel_id=1, source_target_pairs={{0,6},{2,0},{4,2},{6,4},{1,7},{3,1},{5,3},{7,5},{8,14},{10,8},{12,... | collective-permute-start | bytes 1376264 | tf_op jit(solution)/shard_map/gt/ppermute | solution.py:36
  55.9 42.1 %all-to-all-start = ((bf16[16,16,4480]{2,1,0:T(8,128)(2,1)}), bf16[16,16,4480]{2,1,0:T(8,128)(2,1)S(1)}, u32[]{:S(2)}, u32[]{:S(2)}) async-start(bf16[16,16,4480]{2,1,0:T(8,128)(2,1)} %bitcast.24), calls=%async_computation | async-start | bytes 4587520 | tf_op jit(solution)/shard_map/msg/all_to_all | solution.py:697
  63.5 17.4 %collective-permute-start.13 = (bf16[3584,256]{1,0:T(8,128)(2,1)}, bf16[3584,256]{1,0:T(8,128)(2,1)}, u32[]{:S(2)}, u32[]{:S(2)}) collective-permute-start(bf16[3584,256]{1,0:T(8,128)(2,1)} %bitcast.25), channel_id=1, source_target_pairs={{0,1},{1,0},{2,3},{3,2},{4,5},{5,4},{6,7},{7,6},{8,9},{9,8},{10,11... | collective-permute-start | bytes 5505032 | tf_op jit(solution)/shard_map/swap_expert/ppermute | solution.py:45
  89.4 23.5 %collective-permute-start.19 = (bf16[128,3584]{1,0:T(8,128)(2,1)}, bf16[128,3584]{1,0:T(8,128)(2,1)}, u32[]{:S(2)}, u32[]{:S(2)}) collective-permute-start(bf16[128,3584]{1,0:T(8,128)(2,1)} %get-tuple-element.83), channel_id=1, source_target_pairs={{0,2},{2,4},{4,6},{6,0},{1,3},{3,5},{5,7},{7,1},{8,10},{10,12},{12... | collective-permute-start | bytes 2752520 | tf_op jit(solution)/shard_map/part/ppermute | solution.py:41
  89.5 23.4 %collective-permute-start.20 = (bf16[128,3584]{1,0:T(8,128)(2,1)}, bf16[128,3584]{1,0:T(8,128)(2,1)}, u32[]{:S(2)}, u32[]{:S(2)}) collective-permute-start(bf16[128,3584]{1,0:T(8,128)(2,1)} %get-tuple-element.84), channel_id=1, source_target_pairs={{0,6},{2,0},{4,2},{6,4},{1,7},{3,1},{5,3},{7,5},{8,14},{10,8},{12,... | collective-permute-start | bytes 2752520 | tf_op jit(solution)/shard_map/part/ppermute | solution.py:41
  99.3 55.5 %all-to-all-start.1 = ((bf16[16,224,384]{2,1,0:T(8,128)(2,1)}), bf16[16,224,384]{2,1,0:T(8,128)(2,1)S(1)}, u32[]{:S(2)}, u32[]{:S(2)}) async-start(bf16[16,224,384]{2,1,0:T(8,128)(2,1)} %bitcast.20), calls=%async_computation.1 | async-start | bytes 5505024 | tf_op jit(solution)/shard_map/scatter/all_to_all | solution.py:697
  112.9 27.4 %collective-permute-start.22 = (bf16[80,7168]{1,0:T(8,128)(2,1)}, bf16[80,7168]{1,0:T(8,128)(2,1)}, u32[]{:S(2)}, u32[]{:S(2)}) collective-permute-start(bf16[80,7168]{1,0:T(8,128)(2,1)} %get-tuple-element.94), channel_id=1, source_target_pairs={{0,6},{2,4},{4,2},{6,0},{1,7},{3,5},{5,3},{7,1},{8,14},{10,12},{12... | collective-permute-start | bytes 3440648 | tf_op jit(solution)/shard_map/r2/ppermute | solution.py:705
  115.3 25.6 %collective-permute-start.21 = (bf16[80,7168]{1,0:T(8,128)(2,1)}, bf16[80,7168]{1,0:T(8,128)(2,1)}, u32[]{:S(2)}, u32[]{:S(2)}) collective-permute-start(bf16[80,7168]{1,0:T(8,128)(2,1)} %get-tuple-element.85.refs_0_), channel_id=1, source_target_pairs={{0,2},{2,0},{4,6},{6,4},{1,3},{3,1},{5,7},{7,5},{8,10},{10,8},{12,... | collective-permute-start | bytes 3440648 | tf_op jit(solution)/shard_map/r1/ppermute | solution.py:705
  140.9 26.9 %collective-permute-start.25 = (bf16[80,7168]{1,0:T(8,128)(2,1)}, bf16[80,7168]{1,0:T(8,128)(2,1)}, u32[]{:S(2)}, u32[]{:S(2)}) collective-permute-start(bf16[80,7168]{1,0:T(8,128)(2,1)} %get-tuple-element.94), channel_id=1, source_target_pairs={{0,4},{2,6},{4,0},{6,2},{1,5},{3,7},{5,1},{7,3},{8,12},{10,14},{12... | collective-permute-start | bytes 3440648 | tf_op jit(solution)/shard_map/r3/ppermute | solution.py:705
  152.2 48.0 %collective-permute-start.23 = (bf16[80,3584]{1,0:T(8,128)(2,1)}, bf16[80,3584]{1,0:T(8,128)(2,1)S(1)}, u32[]{:S(2)}, u32[]{:S(2)}) collective-permute-start(bf16[80,3584]{1,0:T(8,128)(2,1)} %get-tuple-element.92), channel_id=1, source_target_pairs={{0,2},{2,0},{4,6},{6,4},{1,3},{3,1},{5,7},{7,5},{8,10},{10,8},{12,... | collective-permute-start | bytes 1720328 | tf_op jit(solution)/shard_map/b1/ppermute | solution.py:705
  153.7 46.5 %collective-permute-start.24 = (bf16[80,3584]{1,0:T(8,128)(2,1)}, bf16[80,3584]{1,0:T(8,128)(2,1)}, u32[]{:S(2)}, u32[]{:S(2)}) collective-permute-start(bf16[80,3584]{1,0:T(8,128)(2,1)} %get-tuple-element.93), channel_id=1, source_target_pairs={{0,6},{2,4},{4,2},{6,0},{1,7},{3,5},{5,3},{7,1},{8,14},{10,12},{12... | collective-permute-start | bytes 1720328 | tf_op jit(solution)/shard_map/b2/ppermute | solution.py:705
  160.2 40.0 %all-to-all-start.2 = ((bf16[16,224,384]{2,1,0:T(8,128)(2,1)}), bf16[16,224,384]{2,1,0:T(8,128)(2,1)S(1)}, u32[]{:S(2)}, u32[]{:S(2)}) async-start(bf16[16,224,384]{2,1,0:T(8,128)(2,1)} %grad_sum.1), calls=%async_computation.2 | async-start | bytes 5505024 | tf_op jit(solution)/shard_map/gather/all_to_all | solution.py:697
  176.9 23.4 %collective-permute-start.26 = (bf16[80,3584]{1,0:T(8,128)(2,1)}, bf16[80,3584]{1,0:T(8,128)(2,1)}, u32[]{:S(2)}, u32[]{:S(2)}) collective-permute-start(bf16[80,3584]{1,0:T(8,128)(2,1)} %get-tuple-element.96), channel_id=1, source_target_pairs={{0,4},{2,6},{4,0},{6,2},{1,5},{3,7},{5,1},{7,3},{8,12},{10,14},{12... | collective-permute-start | bytes 1720328 | tf_op jit(solution)/shard_map/b3/ppermute | solution.py:705
  205.5 16.0 %collective-permute-start.27 = (bf16[240,7936]{1,0:T(8,128)(2,1)}, bf16[240,7936]{1,0:T(8,128)(2,1)}, u32[]{:S(2)}, u32[]{:S(2)}) collective-permute-start(bf16[240,7936]{1,0:T(8,128)(2,1)} %get-tuple-element.101.refs_0_), channel_id=1, source_target_pairs={{0,1},{1,0},{2,3},{3,2},{4,5},{5,4},{6,7},{7,6},{8,9},{9,8},{10,11... | collective-permute-start | bytes 11427848 | tf_op jit(solution)/shard_map/swap_bundle/ppermute | solution.py:45
  212.2 22.4 %all-to-all-start.3 = ((bf16[16,8,4480]{2,1,0:T(8,128)(2,1)}), bf16[16,8,4480]{2,1,0:T(8,128)(2,1)}, u32[]{:S(2)}, u32[]{:S(2)}) async-start(bf16[16,8,4480]{2,1,0:T(8,128)(2,1)} %bitcast.23), calls=%async_computation.3 | async-start | bytes 2293760 | tf_op jit(solution)/shard_map/returned/all_to_all | solution.py:697
  216.6 23.2 %collective-permute-start.29 = (bf16[128,3584]{1,0:T(8,128)(2,1)}, bf16[128,3584]{1,0:T(8,128)(2,1)S(1)}, u32[]{:S(2)}, u32[]{:S(2)}) collective-permute-start(bf16[128,3584]{1,0:T(8,128)(2,1)} %get-tuple-element.112), channel_id=1, source_target_pairs={{0,4},{2,6},{4,0},{6,2},{1,5},{3,7},{5,1},{7,3},{8,12},{10,14},{12... | collective-permute-start | bytes 2752520 | tf_op jit(solution)/shard_map/part/ppermute | solution.py:41
  (25 other events, 258.8 us)
